TPU v7x, 256 devices: a whole 4x4x8 slice. The times are simulated.
256 devices in a mesh: dp: 4 (over z_hi), passage: 64 (over z_lo, x, y, core).
Axes of the slice: x: 4, y: 4, z: 8 (z_hi: 4, z_lo: 2; z = z_hi * 2 + z_lo), core: 2. Of those that a mesh axis runs over, the one named last changes fastest.
Arguments:
- question: bfloat16 [8, 32, 4096], P('dp', None, 'passage'), may hold values from -6 to 6
- norm_gain: bfloat16 [4096], P('passage'), may hold values from 0.5 to 1.5
- w_qkv: bfloat16 [4096, 6144], P('passage'), may hold values from -0.09375 to 0.09375
- mem_keys: bfloat16 [128, 8, 200, 2048], P('passage', 'dp'), may hold values from -122 to 122
- mem_values: bfloat16 [128, 8, 200, 2048], P('passage', 'dp'), may hold values from -6 to 6
- mem_length: int32 [128, 8], P('passage', 'dp'), may hold values from 2 to 200
- owner: int32 [128, 4, 2], P('passage', 'dp'), may hold values from 0 to 1, each once within a row
- d_context: bfloat16 [128, 8, 32, 2048], P('passage', 'dp'), may hold values from -0.29882812 to 0.29882812
Outputs:
- context: bfloat16 [128, 8, 32, 2048], P('passage', 'dp')
- d_question: bfloat16 [8, 32, 4096], P('dp', None, 'passage')
- d_gain: float32 [4096], P('passage')
- d_weight: float32 [4096, 6144], P('passage')
Inputs may be any that keep to these rules, and one draw needn't show every extreme that they name: `owner`: the 2 slots of each passage index and group hold one passage of each of the group's questions.
All inputs are finite; a program needn't handle non-finite values.
Results may differ from a plain program's by a relative error of at most 0.015.
The roundings to bfloat16 on the way count: a program that leaves them out, or rounds other values in their place, can miss the bound.
Values may be sent and summed in bfloat16 or wider, within the bound.
No kernel may reach another device: no remote copies, remote signals or barrier semaphores. Data moves between devices by JAX's collectives and lax.ppermute only.
A program may use at most 128 MiB of HBM per device.

v0:
```python
import math

import jax
import jax.numpy as jnp
from jax import lax
from jax.sharding import PartitionSpec as P

D = 4096
HEADS = 32


EPS = 1e-06


def attend(query_rows, key_rows, value_rows, keys_mem, values_mem, length, d_out_rows):
    slots, qlen, inner = query_rows.shape
    head_dim = inner // HEADS
    scale = 1.0 / math.sqrt(head_dim)
    total = qlen + keys_mem.shape[1]
    keys = jnp.concatenate([key_rows, keys_mem], axis=1).reshape(slots, total, HEADS, head_dim)
    values = jnp.concatenate([value_rows, values_mem], axis=1).reshape(
        slots, total, HEADS, head_dim
    )
    query = query_rows.reshape(slots, qlen, HEADS, head_dim)
    scores = jnp.einsum("sqhd,skhd->shqk", query, keys, preferred_element_type=jnp.float32) * scale
    position = jnp.arange(total, dtype=jnp.int32)
    live = (position[None, :] < (length + qlen)[:, None])[:, None, None, :]
    masked = jnp.where(live, scores, -1e30)
    top = jnp.max(masked, axis=-1, keepdims=True)
    expo = jnp.where(live, jnp.exp(masked - top), 0.0)
    prob = expo / jnp.sum(expo, axis=-1, keepdims=True)
    prob_b = prob.astype(jnp.bfloat16)
    context = jnp.einsum("shqk,skhd->sqhd", prob_b, values, preferred_element_type=jnp.float32)
    context = context.reshape(slots, qlen, inner).astype(jnp.bfloat16)
    d_out = d_out_rows.reshape(slots, qlen, HEADS, head_dim)
    d_prob = jnp.einsum("sqhd,skhd->shqk", d_out, values, preferred_element_type=jnp.float32)
    inner_sum = jnp.sum(d_prob * prob, axis=-1, keepdims=True)
    d_scores = (prob * (d_prob - inner_sum) * scale).astype(jnp.bfloat16)
    d_query = jnp.einsum("shqk,skhd->sqhd", d_scores, keys, preferred_element_type=jnp.float32)
    d_key = jnp.einsum(
        "shqk,sqhd->skhd", d_scores[..., :qlen], query, preferred_element_type=jnp.float32
    )
    d_value = jnp.einsum(
        "shqk,sqhd->skhd", prob_b[..., :qlen], d_out, preferred_element_type=jnp.float32
    )
    grads = jnp.concatenate(
        [
            d_query.reshape(slots, qlen, inner),
            d_key.reshape(slots, qlen, inner),
            d_value.reshape(slots, qlen, inner),
        ],
        axis=-1,
    )
    return (context, grads)


def shards(question, norm_gain, w_qkv, mem_keys, mem_values, mem_length, owner, d_context):
    count, qlen, width = question.shape
    local_passages = mem_keys.shape[0]
    memlen = mem_keys.shape[2]
    inner = mem_keys.shape[-1]
    total_rows = count * qlen
    inputs = question.astype(jnp.float32)
    squares = lax.psum(jnp.sum(inputs * inputs, axis=-1), "passage")
    rate = lax.rsqrt(squares / D + EPS)
    rate_rows = rate.reshape(total_rows, 1)
    gain = norm_gain.astype(jnp.float32)
    flat_inputs = inputs.reshape(total_rows, width)
    scaled = (flat_inputs * gain).astype(jnp.bfloat16)
    partial_pre = jnp.dot(scaled, w_qkv, preferred_element_type=jnp.float32)
    pre = lax.psum(partial_pre, "passage")
    qkv = (pre * rate_rows).astype(jnp.bfloat16)
    qkv = qkv.reshape(count, qlen, 3 * inner)
    slots = local_passages * count
    slot_owner = owner.reshape(slots)
    rows = jnp.take(qkv, slot_owner, axis=0)
    context, grads = attend(
        rows[..., :inner],
        rows[..., inner : 2 * inner],
        rows[..., 2 * inner :],
        mem_keys.reshape(slots, memlen, inner),
        mem_values.reshape(slots, memlen, inner),
        mem_length.reshape(slots),
        d_context.reshape(slots, qlen, inner),
    )
    onehot = (slot_owner[:, None] == jnp.arange(count, dtype=jnp.int32)[None, :]).astype(
        jnp.float32
    )
    local_grad = jnp.einsum("sc,slf->clf", onehot, grads, precision=lax.Precision.HIGHEST)
    local_grad = local_grad.reshape(total_rows, 3 * inner)
    grad = lax.psum(local_grad, "passage")
    d_rate = jnp.sum(grad * pre, axis=-1)
    d_pre = (grad * rate_rows).astype(jnp.bfloat16)
    d_input = jnp.dot(d_pre, w_qkv.T, preferred_element_type=jnp.float32)
    local_weight = jnp.dot(scaled.T, d_pre, preferred_element_type=jnp.float32)
    local_gain = jnp.sum(flat_inputs * d_input, axis=0)
    d_weight, d_gain = (
        lax.psum(local_weight.astype(jnp.bfloat16), "dp").astype(jnp.float32),
        lax.psum(local_gain.astype(jnp.bfloat16), "dp").astype(jnp.float32),
    )
    cubed = d_rate * rate.reshape(total_rows) ** 3
    d_question = (gain * d_input - cubed[:, None] * flat_inputs / D).astype(jnp.bfloat16)
    return (
        context.reshape(local_passages, count, qlen, inner),
        d_question.reshape(count, qlen, width),
        d_gain,
        d_weight,
    )


def solution(mesh):
    return jax.shard_map(
        shards,
        mesh=mesh,
        in_specs=(
            P("dp", None, "passage"),
            P("passage"),
            P("passage", None),
            P("passage", "dp", None, None),
            P("passage", "dp", None, None),
            P("passage", "dp"),
            P("passage", "dp", None),
            P("passage", "dp", None, None),
        ),
        out_specs=(
            P("passage", "dp", None, None),
            P("dp", None, "passage"),
            P("passage"),
            P("passage", None),
        ),
        check_vma=False,
    )
```

profile of v0, /device:TPU:1, one launch (start us, length us, event | category | flops | bytes accessed | tf_op | source)
XLA Modules:
  0.0 1270.6 jit_solution(5888826545219158145)
XLA Ops:
  10.2 6.0 copy.24
  16.4 141.3 %psum.36 = f32[2,32]{1,0:T(2,128)S(1)} all-reduce(f32[2,32]{1,0:T(2,128)S(1)} %fusion.29), channel_id=1, replica_groups=mesh['dp'=4,'passage'=64] {'passage'}, use_global_device_ids=true, to_apply=%region_2.0 | all-reduce | flops 64 | bytes 512 | tf_op jit(solution)/shard_map/psum | solution.py:64
  159.2 6.0 copy.22
  165.2 2.1 reshape_reshape.3
  167.4 401.6 %all-reduce.4.cloned.1.call-done = f32[64,6144]{1,0:T(8,128)} async-done(((f32[64,6144]{1,0:T(8,128)}), f32[64,6144]{1,0:T(8,128)}) %all-reduce.4.cloned.1.call-update) | async-done | bytes 1572880 | tf_op jit(solution)/shard_map/psum | solution.py:71
  574.4 2.8 reshape.134
  578.9 4.5 fusion.17
  586.1 2.2 copy-done.2
  588.6 2.1 fusion.18
  590.7 22.7 %fusion.4 = bf16[4,32,32,232]{3,2,1,0:T(8,128)(2,1)S(1)} fusion(f32[4,32,232,32]{2,3,1,0:T(8,128)S(1)} %fusion.18, f32[4,32,32,232]{3,2,1,0:T(8,128)S(1)} %get-tuple-element.10, f32[4,32,32]{2,1,0:T(8,128)S(1)} %get-tuple-element.9), kind=kOutput, calls=%fused_computation.10 | output fusion | flops 6656231 | bytes 9519104 | tf_op jit(solution)/shard_map/sub | solution.py:38
  613.4 2.0 convolution_bitcast_fusion.1
  616.4 3.2 fusion.20
  623.2 4.3 copy.42
  627.5 3.0 reshape.150
  630.5 2.5 copy.41
  633.1 2.5 reshape.149
  635.5 5.0 fusion.6
  640.5 2.1 copy.38
  642.6 555.5 %all-reduce.6.cloned.1.call-done = f32[64,6144]{1,0:T(8,128)} async-done(((f32[64,6144]{1,0:T(8,128)}), f32[64,6144]{1,0:T(8,128)}) %all-reduce.6.cloned.1.call-update) | async-done | bytes 1572880 | tf_op jit(solution)/shard_map/psum | solution.py:91
  1198.1 2.7 convolution_convert_fusion
  1200.9 4.7 fusion.22
  1210.3 11.6 psum.38
  1222.5 39.2 %all-reduce.8.cloned.1.call-done = bf16[64,6144]{1,0:T(8,128)(2,1)} async-done(((bf16[64,6144]{1,0:T(8,128)(2,1)}), bf16[64,6144]{1,0:T(8,128)(2,1)}) %all-reduce.8.cloned.1.call-update) | async-done | bytes 786448 | tf_op jit(solution)/shard_map/psum | solution.py:98
  1261.6 2.4 convert_element_type.61
  (66 shorter events, 24.8 us)
Async XLA Ops:
  7.2 1.5 copy-start
  7.2 561.8 %all-reduce.4.cloned.1.call-start = ((), (), s32[]{:S(2)}) async-start(), calls=%async_computation | async-start | bytes 3145728 | tf_op jit(solution)/shard_map/psum | solution.py:71
  10.2 6.1 copy-start.11
  10.2 147.6 %copy-start.12 = (s32[2,1,2]{2,1,0:T(1,128)S(1)}, s32[2,1,2]{2,1,0:T(1,128)}, u32[]{:S(2)}) copy-start(s32[2,1,2]{2,1,0:T(1,128)} %param.14) | copy-start | bytes 52
  10.2 148.9 %copy-start.13 = (s32[2,2]{1,0:T(2,128)S(1)}, s32[2,2]{1,0:T(2,128)}, u32[]{:S(2)}) copy-start(s32[2,2]{1,0:T(2,128)} %param.13) | copy-start | bytes 52
  10.2 1187.9 %all-reduce.6.cloned.1.call-start = ((), (), s32[]{:S(2)}) async-start(), calls=%async_computation.1 | async-start | bytes 3145728 | tf_op jit(solution)/shard_map/psum | solution.py:91
  16.3 148.9 %copy-start.10 = (bf16[2,2,32,2048]{3,2,1,0:T(8,128)(2,1)S(1)}, bf16[2,2,32,2048]{3,2,1,0:T(8,128)(2,1)}, u32[]{:S(2)}) copy-start(bf16[2,2,32,2048]{3,2,1,0:T(8,128)(2,1)} %param.15) | copy-start | bytes 1572868
  583.4 2.7 copy-start.7
  585.4 2.9 copy-start.2
  585.4 3.2 copy-start.5
  586.1 33.4 %copy-start.9 = (bf16[4,32,32,232]{3,2,1,0:T(8,128)(2,1)}, bf16[4,32,32,232]{3,2,1,0:T(8,128)(2,1)S(1)}, u32[]{:S(2)}) copy-start(bf16[4,32,32,232]{3,2,1,0:T(8,128)(2,1)S(1)} %fusion.49) | copy-start | bytes 5701636
  590.7 22.7 %copy-start.4 = (bf16[4,32,32,64]{3,2,1,0:T(8,128)(2,1)S(1)}, bf16[4,32,32,64]{3,2,1,0:T(8,128)(2,1)}, u32[]{:S(2)}) copy-start(bf16[4,32,32,64]{3,2,1,0:T(8,128)(2,1)} %reshape.134) | copy-start | bytes 1572868
  613.4 2.9 copy-start.1
  623.2 7.3 copy-start.6
  640.5 560.3 %copy-start.8 = (bf16[4,32,2048]{1,2,0:T(8,128)(2,1)S(1)}, bf16[4,32,2048]{1,2,0:T(8,128)(2,1)}, u32[]{:S(2)}) copy-start(bf16[4,32,2048]{1,2,0:T(8,128)(2,1)} %copy.21) | copy-start | bytes 1572868
  642.6 619.0 %all-reduce.8.cloned.1.call-start = ((), (), s32[]{:S(2)}) async-start(), calls=%async_computation.2 | async-start | bytes 1572864 | tf_op jit(solution)/shard_map/psum | solution.py:98
  1205.6 2.0 copy-start.3
Sparse Core Ops, SparseCore 0:
  11.2 557.7 all-reduce.3
  642.7 555.3 all-reduce.5
  1201.4 60.2 all-reduce.7
where the time goes:
time: 1270 us
  waiting for transfers between devices  996 us (78%)
  blocking collectives  153 us (12%)
  local copies, waits for them, and re-layouts  46.1 us (4%)
  other arithmetic  34 us (3%)
  matrix products  27.2 us (2%)
  between operations  14 us (1%)
    psum x1, waiting for transfers between devices, shards(): grad = lax.psum(local_grad, 'passage')  555 us
    psum x1, waiting for transfers between devices, shards(): pre = lax.psum(partial_pre, 'passage')  402 us
    psum x1, blocking collectives, shards(): squares = lax.psum(jnp.sum(inputs * inputs, axis=-1), 'passage')  141 us
    psum x1, waiting for transfers between devices, shards(): lax.psum(local_weight.astype(jnp.bfloat16), 'dp').astype(jnp.float32)  39.2 us
  transfers between devices with their start and end apart: 3, of which 3 were waited for; matrix products, arithmetic and copies ran while one was open for 2% of the time, Pallas kernels for 0%

commit v1 on v0

v1 whole, which is shorter than its diff:
```python
import functools

import jax
import jax.numpy as jnp
from jax import lax
from jax.experimental import pallas as pl
from jax.experimental.pallas import tpu as pltpu
from jax.sharding import PartitionSpec as P

D = 4096
EPS = 1e-06
QLEN = 32
ROWS = 64
FEATS = 64
MEM = 200
HALF = 1024
COLS = 3 * HALF
CHIPS = 32
COL_BLOCKS = 8
CHUNK = 48
K_AT, V_AT, PACKED = 32, 240, 448
FOLD = 0.125

BF16 = jnp.bfloat16
F32 = jnp.float32
VMEM = pl.BlockSpec(memory_space=pltpu.VMEM)
SMEM = pl.BlockSpec(memory_space=pltpu.SMEM)
PARAMS = pltpu.CompilerParams(vmem_limit_bytes=24 * 1024 * 1024)

NT = (((1,), (1,)), ((), ()))
TN = (((0,), (0,)), ((), ()))


def dot(a, b, dims=(((1,), (0,)), ((), ()))):
    return lax.dot_general(a, b, dims, preferred_element_type=F32)


def lanes_of(index, width):
    return pl.ds(pl.multiple_of(index * width, width), width)


def pack_w(core, w_ref, q_ref, gain_ref, out_ref):
    other = 1 - core[0]
    for b in range(3):
        out_ref[0:FEATS, b * HALF : (b + 1) * HALF] = w_ref[:, lanes_of(2 * b + other, HALF)]
    for j in range(4):
        out_ref[64:80, j * 128 : j * 128 + 64] = q_ref[j * 16 : (j + 1) * 16, :]
    out_ref[64:80, 512:576] = jnp.broadcast_to(gain_ref[...], (16, FEATS))


def pack_memory(core, keys_ref, values_ref, d_ref, out_ref):
    out_ref[0, 0:QLEN] = d_ref[0, 0]
    out_ref[0, K_AT : K_AT + MEM] = keys_ref[0, 0]
    out_ref[0, V_AT : V_AT + MEM] = values_ref[0, 0]


def project(core, w_ref, q_ref, gain_ref, recv_ref, part_ref, wc_ref, pair_ref, gains_ref):
    theirs = jnp.concatenate(
        [recv_ref[64:80, j * 128 : j * 128 + 64].astype(F32) for j in range(4)], axis=0
    )
    pair = jnp.concatenate([q_ref[...].astype(F32), theirs], axis=1)
    gains = jnp.concatenate(
        [gain_ref[...].astype(F32), recv_ref[64:80, 512:576].astype(F32)[0:1]], axis=1
    )
    pair_ref[...] = pair.astype(BF16)
    gains_ref[...] = gains
    scaled = (pair * gains).astype(BF16)
    for b in range(3):
        wc_ref[0:FEATS, b * HALF : (b + 1) * HALF] = w_ref[:, lanes_of(2 * b + core[0], HALF)]
    wc_ref[FEATS:, :] = recv_ref[0:FEATS, :]
    for cb in range(COL_BLOCKS):
        pre = dot(scaled, wc_ref[:, cb * 384 : (cb + 1) * 384])
        for rb in range(4):
            for t in range(3):
                part_ref[rb * COL_BLOCKS + cb, t * 16 : (t + 1) * 16, :] = pre[
                    rb * 16 : (rb + 1) * 16, t * 128 : (t + 1) * 128
                ]
    squares = jnp.sum(pair * pair, axis=1, keepdims=True)
    low = lax.broadcasted_iota(jnp.int32, (8, 128), 1) < 64
    for rb in range(4):
        tile = jnp.where(
            low, squares[rb * 16 : rb * 16 + 8], squares[rb * 16 + 8 : rb * 16 + 16]
        )
        for cb in range(COL_BLOCKS):
            part_ref[rb * COL_BLOCKS + cb, CHUNK : CHUNK + 8, :] = tile


def normalise(part_ref, qkv_ref, pre_ref, rate_ref):
    total = jnp.sum(part_ref[...], axis=0)
    rates = lax.rsqrt(total[CHUNK:] / D + EPS)
    rate = jnp.concatenate([rates[:, 0:1], rates[:, 64:65]], axis=0)
    rate = jnp.broadcast_to(rate, (16, 128))
    pre = total[:CHUNK]
    pre_ref[...] = pre
    rate_ref[...] = rate
    qkv = (pre * jnp.concatenate([rate] * 3, axis=0)).astype(BF16)
    for k in range(CHIPS):
        qkv_ref[k] = qkv


def attend(
    own, oth, qkv_ref, keys_ref, values_ref, d_ref, packed_ref, ctx_own, ctx_oth, grad_ref,
    rows, mask_q, mask_d, kcat, vcat,
):
    step = pl.program_id(0)

    @pl.when(step == 0)
    def _():
        for k in range(CHIPS):
            rb, cb = divmod(k, COL_BLOCKS)
            for t in range(3):
                at = (cb * 3 + t) * 128
                rows[rb * 16 : (rb + 1) * 16, at : at + 128] = qkv_ref[k, t * 16 : (t + 1) * 16, :]
        grad_ref[...] = jnp.zeros_like(grad_ref)
        head = lax.broadcasted_iota(jnp.int32, (128, 256), 0) // QLEN
        lane = lax.broadcasted_iota(jnp.int32, (128, 256), 1) // 64
        same = jnp.where(head == lane, 1.0, 0.0)
        mask_d[...] = same.astype(BF16)
        mask_q[...] = (same * FOLD).astype(BF16)
        for unit in range(8):
            kcat[unit, 224:256] = jnp.zeros((32, 256), BF16)
            vcat[unit, 224:256] = jnp.zeros((32, 256), BF16)

    key_at = lax.broadcasted_iota(jnp.int32, (1, 256), 1)
    lane_head = lax.broadcasted_iota(jnp.int32, (QLEN, 256), 1) // 64

    def diagonal(full):
        out = full[0:QLEN]
        for h in range(1, 4):
            out = jnp.where(lane_head == h, full[h * QLEN : (h + 1) * QLEN], out)
        return out

    for side, info in enumerate((own, oth)):
        live = key_at < info[step] + QLEN
        question = info[4 + step]
        at = pl.ds(pl.multiple_of(question * QLEN, QLEN), QLEN)
        for hg in range(4):
            unit = side * 4 + hg
            lanes = slice(hg * 256, (hg + 1) * 256)
            kc, vc = kcat.at[unit], vcat.at[unit]
            kc[0:QLEN] = rows[at, HALF + hg * 256 : HALF + (hg + 1) * 256]
            vc[0:QLEN] = rows[at, 2 * HALF + hg * 256 : 2 * HALF + (hg + 1) * 256]
            if side == 0:
                kc[QLEN : QLEN + MEM] = keys_ref[0, 0, :, lanes]
                vc[QLEN : QLEN + MEM] = values_ref[0, 0, :, lanes]
                d_out = d_ref[0, 0, :, lanes]
            else:
                kc[QLEN : QLEN + MEM] = packed_ref[0, K_AT : K_AT + MEM, lanes]
                vc[QLEN : QLEN + MEM] = packed_ref[0, V_AT : V_AT + MEM, lanes]
                d_out = packed_ref[0, 0:QLEN, lanes]
            keys, values = kc[...], vc[...]
            query = jnp.concatenate([rows[at, lanes]] * 4, axis=0) * mask_q[...]
            d_rows = jnp.concatenate([d_out] * 4, axis=0) * mask_d[...]
            scores = jnp.where(live, dot(query, keys, NT), -1e30)
            d_prob = dot(d_rows, values, NT)
            expo = jnp.exp(scores - jnp.max(scores, axis=1, keepdims=True))
            prob = expo * (1.0 / jnp.sum(expo, axis=1, keepdims=True))
            inner = jnp.sum(d_prob * prob, axis=1, keepdims=True)
            prob_b = prob.astype(BF16)
            d_scores = (prob * (d_prob - inner)).astype(BF16)
            context = diagonal(dot(prob_b, values)).astype(BF16)
            if side == 0:
                ctx_own[0, :, lanes] = context
            else:
                ctx_oth[0, :, lanes] = context
            grads = (
                diagonal(dot(d_scores, keys)) * FOLD,
                dot(d_scores[:, 0:QLEN], query, TN),
                dot(prob_b[:, 0:QLEN], d_rows, TN),
            )
            for part, grad in enumerate(grads):
                for tt in range(2):
                    cb, t = divmod(part * 8 + hg * 2 + tt, 3)
                    for r in range(2):
                        k = (2 * question + r) * COL_BLOCKS + cb
                        grad_ref[k, t * 16 : (t + 1) * 16, :] += grad[
                            r * 16 : (r + 1) * 16, tt * 128 : (tt + 1) * 128
                        ]


def split_rows(value):
    high = value.astype(BF16).astype(F32)
    low = lax.broadcasted_iota(jnp.int32, value.shape, 1) < 64
    return jnp.where(low, high, value - high).astype(BF16)


def finish_grad(recv_ref, pre_ref, rate_ref, pair_ref, out_ref, cubed_ref):
    grad = jnp.sum(recv_ref[...], axis=0)
    rate = rate_ref[...]
    product = grad * pre_ref[...]
    product = product[0:16] + product[16:32] + product[32:48]
    d_rate = jnp.sum(product, axis=1, keepdims=True)
    cubed_ref[...] = split_rows(d_rate * rate * rate * rate)
    d_pre = (grad * jnp.concatenate([rate] * 3, axis=0)).astype(BF16)
    for g in range(4):
        out_ref[g, 0:CHUNK] = d_pre
        out_ref[g, CHUNK:] = pair_ref[...]


def spread(recv_ref, cubed_ref, out_ref):
    for k in range(CHIPS):
        for g in range(4):
            out_ref[k, g * CHUNK : (g + 1) * CHUNK] = recv_ref[g, 0:CHUNK]
        out_ref[k, 4 * CHUNK :] = cubed_ref[...]


def weight_grads(
    group, recv_ref, groups_ref, gains_ref, wc_ref, own_ref, send_ref, small_ref, d_in, d_pre
):
    pairs = jnp.concatenate([groups_ref[g, CHUNK:] for g in range(4)], axis=0).astype(F32)
    scaled_t = (pairs * gains_ref[...]).T.astype(BF16)
    for cb in range(COL_BLOCKS):
        for rb in range(4):
            for g in range(4):
                for t in range(3):
                    d_pre[
                        cb, g * ROWS + rb * 16 : g * ROWS + (rb + 1) * 16, t * 128 : (t + 1) * 128
                    ] = recv_ref[
                        rb * COL_BLOCKS + cb, g * CHUNK + t * 16 : g * CHUNK + (t + 1) * 16, :
                    ]
        block = d_pre[cb]
        at = slice(cb * 384, (cb + 1) * 384)
        d_w = dot(scaled_t, block)
        own_ref[:, at] = d_w[0:FEATS]
        send_ref[:, at] = d_w[FEATS:].astype(BF16)
        term = dot(block, wc_ref[:, at], NT)
        if cb == 0:
            d_in[...] = term
        else:
            d_in[...] += term
    cubed = []
    for rb in range(4):
        total = jnp.zeros((16, 128), F32)
        for cb in range(COL_BLOCKS):
            total += recv_ref[rb * COL_BLOCKS + cb, 4 * CHUNK :].astype(F32)
        cubed.append(total[:, 0:1] + total[:, 64:65])
    cubed = jnp.broadcast_to(jnp.concatenate(cubed, axis=0), (ROWS, 128))
    mine = d_in[pl.ds(pl.multiple_of(group[0] * ROWS, ROWS), ROWS), :]
    d_gain = jnp.sum(pairs * d_in[...], axis=0, keepdims=True)
    low = lax.broadcasted_iota(jnp.int32, (ROWS, 128), 1) < 64
    small_ref[0, 0:ROWS] = mine
    small_ref[0, ROWS : ROWS + 8] = jnp.broadcast_to(d_gain, (8, 128))
    small_ref[1, 0:ROWS] = jnp.where(low, cubed, mine)
    small_ref[1, ROWS : ROWS + 8] = jnp.broadcast_to(d_gain, (8, 128))


def write_weight(core, own_ref, recv_ref, out_ref):
    half = pl.program_id(0) % 2

    @pl.when(half == core[0])
    def _():
        out_ref[...] = own_ref[...]

    @pl.when(half != core[0])
    def _():
        out_ref[...] = recv_ref[...].astype(F32)


def finish_small(small_ref, recv_ref, q_ref, gain_ref, dq_ref, dg_ref):
    d_input = small_ref[0:ROWS, 0:FEATS] + recv_ref[0:ROWS, 64:128]
    cubed = small_ref[ROWS + 8 :, 0:1] + recv_ref[0:ROWS, 0:1]
    question = q_ref[...].astype(F32)
    gain = gain_ref[...].astype(F32)
    dq_ref[...] = (gain * d_input - cubed * question / D).astype(BF16)
    dg_ref[...] = small_ref[ROWS : ROWS + 1, 0:FEATS] + recv_ref[ROWS : ROWS + 1, 64:128]


def call(body, outs, specs, scratch=()):
    return pl.pallas_call(
        body,
        out_shape=[jax.ShapeDtypeStruct(s, t) for s, t in outs],
        in_specs=specs,
        out_specs=[VMEM] * len(outs),
        scratch_shapes=list(scratch),
        compiler_params=PARAMS,
    )


def shards(question, norm_gain, w_qkv, mem_keys, mem_values, mem_length, owner, d_context):
    position = lax.axis_index("passage")
    core = jnp.reshape(position % 2, (1,)).astype(jnp.int32)
    group = jnp.reshape(lax.axis_index("dp"), (1,)).astype(jnp.int32)
    swap = [(i, i ^ 1) for i in range(2 * CHIPS)]
    same_core = [[c + 2 * i for i in range(CHIPS)] for c in range(2)]

    def exchange(x):
        return lax.all_to_all(x, "passage", 0, 0, tiled=True, axis_index_groups=same_core)

    q64 = question.reshape(ROWS, FEATS)
    gain = norm_gain.reshape(1, FEATS)

    (sent,) = call(pack_w, [((80, COLS), BF16)], [SMEM] + [VMEM] * 3)(core, w_qkv, q64, gain)
    recv = lax.ppermute(sent, "passage", swap)

    info = jnp.concatenate([mem_length.reshape(4), owner.reshape(4)])
    other_info = lax.ppermute(info, "passage", swap)
    packed = pl.pallas_call(
        pack_memory,
        out_shape=jax.ShapeDtypeStruct((4, PACKED, HALF), BF16),
        grid_spec=pltpu.PrefetchScalarGridSpec(
            num_scalar_prefetch=1,
            grid=(4,),
            in_specs=[
                pl.BlockSpec((1, 1, MEM, HALF), lambda s, c: (s // 2, s % 2, 0, 1 - c[0])),
                pl.BlockSpec((1, 1, MEM, HALF), lambda s, c: (s // 2, s % 2, 0, 1 - c[0])),
                pl.BlockSpec((1, 1, QLEN, HALF), lambda s, c: (s // 2, s % 2, 0, 1 - c[0])),
            ],
            out_specs=pl.BlockSpec((1, PACKED, HALF), lambda s, c: (s, 0, 0)),
        ),
        compiler_params=PARAMS,
    )(core, mem_keys, mem_values, d_context)
    packed = lax.ppermute(packed, "passage", swap)

    part, wc, pair, gains = call(
        project,
        [
            ((CHIPS, CHUNK + 8, 128), F32),
            ((2 * FEATS, COLS), BF16),
            ((ROWS, 2 * FEATS), BF16),
            ((1, 2 * FEATS), F32),
        ],
        [SMEM] + [VMEM] * 4,
    )(core, w_qkv, q64, gain, recv)
    part = exchange(part)
    qkv, pre, rate = call(
        normalise,
        [((CHIPS, CHUNK, 128), BF16), ((CHUNK, 128), F32), ((16, 128), F32)],
        [VMEM],
    )(part)
    qkv = exchange(qkv)

    own_info = jnp.concatenate([info, core])
    ctx_own, ctx_oth, grads = pl.pallas_call(
        attend,
        out_shape=[
            jax.ShapeDtypeStruct((4, QLEN, HALF), BF16),
            jax.ShapeDtypeStruct((4, QLEN, HALF), BF16),
            jax.ShapeDtypeStruct((CHIPS, CHUNK, 128), F32),
        ],
        grid_spec=pltpu.PrefetchScalarGridSpec(
            num_scalar_prefetch=2,
            grid=(4,),
            in_specs=[
                pl.BlockSpec((CHIPS, CHUNK, 128), lambda s, c, o: (0, 0, 0)),
                pl.BlockSpec((1, 1, MEM, HALF), lambda s, c, o: (s // 2, s % 2, 0, c[8])),
                pl.BlockSpec((1, 1, MEM, HALF), lambda s, c, o: (s // 2, s % 2, 0, c[8])),
                pl.BlockSpec((1, 1, QLEN, HALF), lambda s, c, o: (s // 2, s % 2, 0, c[8])),
                pl.BlockSpec((1, PACKED, HALF), lambda s, c, o: (s, 0, 0)),
            ],
            out_specs=[
                pl.BlockSpec((1, QLEN, HALF), lambda s, c, o: (s, 0, 0)),
                pl.BlockSpec((1, QLEN, HALF), lambda s, c, o: (s, 0, 0)),
                pl.BlockSpec((CHIPS, CHUNK, 128), lambda s, c, o: (0, 0, 0)),
            ],
            scratch_shapes=[
                pltpu.VMEM((ROWS, COLS), BF16),
                pltpu.VMEM((128, 256), BF16),
                pltpu.VMEM((128, 256), BF16),
                pltpu.VMEM((8, 256, 256), BF16),
                pltpu.VMEM((8, 256, 256), BF16),
            ],
        ),
        compiler_params=PARAMS,
    )(own_info, other_info, qkv, mem_keys, mem_values, d_context, packed)
    ctx_mine = lax.ppermute(ctx_oth, "passage", swap)
    first = core[0] == 0
    context = jnp.concatenate(
        [jnp.where(first, ctx_own, ctx_mine), jnp.where(first, ctx_mine, ctx_own)], axis=-1
    )

    grads = exchange(grads)
    chunk, cubed = call(
        finish_grad,
        [((4, CHUNK + ROWS, 128), BF16), ((16, 128), BF16)],
        [VMEM] * 4,
    )(grads, pre, rate, pair)
    groups = lax.all_to_all(chunk, "dp", 0, 0, tiled=True)
    (d_pre,) = call(spread, [((CHIPS, 4 * CHUNK + 16, 128), BF16)], [VMEM] * 2)(groups, cubed)
    d_pre = exchange(d_pre)
    own_w, send_w, small = call(
        weight_grads,
        [((FEATS, COLS), F32), ((FEATS, COLS), BF16), ((2, ROWS + 8, 128), F32)],
        [SMEM] + [VMEM] * 4,
        [pltpu.VMEM((4 * ROWS, 128), F32), pltpu.VMEM((COL_BLOCKS, 4 * ROWS, 384), BF16)],
    )(group, d_pre, groups, gains, wc)
    recv_w = lax.ppermute(send_w, "passage", swap)
    recv_small = lax.ppermute(small[1], "passage", swap)
    own_small = jnp.concatenate([small[0], small[1, 0:ROWS]], axis=0)
    d_question, d_gain = call(
        finish_small, [((ROWS, FEATS), BF16), ((1, FEATS), F32)], [VMEM] * 4
    )(own_small, recv_small, q64, gain)
    d_weight = pl.pallas_call(
        write_weight,
        out_shape=jax.ShapeDtypeStruct((FEATS, 2 * COLS), F32),
        grid_spec=pltpu.PrefetchScalarGridSpec(
            num_scalar_prefetch=1,
            grid=(6,),
            in_specs=[
                pl.BlockSpec((FEATS, HALF), lambda j, c: (0, j // 2)),
                pl.BlockSpec((FEATS, HALF), lambda j, c: (0, j // 2)),
            ],
            out_specs=pl.BlockSpec((FEATS, HALF), lambda j, c: (0, j)),
        ),
        compiler_params=PARAMS,
    )(core, own_w, recv_w)
    return (
        context.reshape(2, 2, QLEN, 2 * HALF),
        d_question.reshape(question.shape),
        d_gain.reshape(norm_gain.shape),
        d_weight,
    )


def solution(mesh):
    return jax.shard_map(
        shards,
        mesh=mesh,
        in_specs=(
            P("dp", None, "passage"),
            P("passage"),
            P("passage", None),
            P("passage", "dp", None, None),
            P("passage", "dp", None, None),
            P("passage", "dp"),
            P("passage", "dp", None),
            P("passage", "dp", None, None),
        ),
        out_specs=(
            P("passage", "dp", None, None),
            P("dp", None, "passage"),
            P("passage"),
            P("passage", None),
        ),
        check_vma=False,
    )
```

time: 1270 us -> 148 us (0.12)
  waiting for transfers between devices: 996 us -> 23.2 us
  blocking collectives: 153 us -> 50.3 us
  local copies, waits for them, and re-layouts: 46.1 us -> 14.1 us
  other arithmetic: 34 us -> 3.15 us
  Pallas kernels: 0 us -> 28 us
  starting transfers between devices: 0.12 us -> 27.4 us
  matrix products: 27.2 us -> 0 us
  between operations: 14 us -> 0.81 us
    psum x3 -> x0, waiting for transfers between devices: 996 us -> none  [the longest x1 555 us: shards(): grad = lax.psum(local_grad, 'passage')]
    psum x2 -> x0, blocking collectives: 153 us -> none  [the longest x1 141 us: shards(): squares = lax.psum(jnp.sum(inputs * inputs, axis=-1), 'passage')]
    all_to_all x0 -> x3, blocking collectives: none -> 50.3 us  [the longest x2 35.9 us: exchange(): lax.all_to_all(x, 'passage', 0, 0, tiled=True, axis_index_groups=same_core)]
    pallas_call x0 -> x10, Pallas kernels: none -> 28 us  [the longest x1 19.2 us: shards(): pl.pallas_call(attend, out_shape=[jax.ShapeDtypeStruct((4, QLEN, HALF), B...]
    dot_general x10 -> x0, matrix products: 27.2 us -> none  [the longest x1 4.95 us: shards(): jnp.einsum('sc,slf->clf', onehot, grads, precision=lax.Precision.HIGHEST)]
    sub x2 -> x0, other arithmetic: 24.6 us -> none  [the longest x1 22.7 us: attend(): d_scores = (prob * (d_prob - inner_sum) * scale).astype(jnp.bfloat16)]
    reshape x9 -> x2, local copies, waits for them, and re-layouts: 18.3 us -> 0.17 us  [shards(): info = jnp.concatenate([mem_length.reshape(4), owner.reshape(4)])]
    ppermute x0 -> x6, starting transfers between devices: none -> 16.7 us  [the longest x1 6.95 us: shards(): recv_w = lax.ppermute(send_w, 'passage', swap)]
  transfers between devices with their start and end apart: 3 -> 8, of which waited for: 3 -> 6; matrix products, arithmetic and copies ran while one was open for 2% -> 3% of each run, Pallas kernels for 0% -> 1%
where the time goes in v1:
time: 148 us; the launch traced here: 147 us
  blocking collectives  50.3 us (34%)
  Pallas kernels  28 us (19%)
  starting transfers between devices  27.4 us (19%)
  waiting for transfers between devices  23.2 us (16%)
  local copies, waits for them, and re-layouts  14.1 us (10%)
  other arithmetic  3.15 us (2%)
    all_to_all x2, blocking collectives, exchange(): lax.all_to_all(x, 'passage', 0, 0, tiled=True, axis_index_groups=same_core)  35.9 us
    pallas_call x1, Pallas kernels, shards(): pl.pallas_call(attend, out_shape=[jax.ShapeDtypeStruct((4, QLEN, HALF), B...  19.2 us
    all_to_all x1, blocking collectives, shards(): groups = lax.all_to_all(chunk, 'dp', 0, 0, tiled=True)  14.4 us
    all_to_all x2, waiting for transfers between devices, exchange(): lax.all_to_all(x, 'passage', 0, 0, tiled=True, axis_index_groups=same_core)  14.1 us
    unnamed x59, local copies, waits for them, and re-layouts  13.9 us
    all_to_all x2, starting transfers between devices, exchange(): lax.all_to_all(x, 'passage', 0, 0, tiled=True, axis_index_groups=same_core)  10.7 us
    ppermute x1, starting transfers between devices, shards(): recv_w = lax.ppermute(send_w, 'passage', swap)  6.95 us
    ppermute x1, waiting for transfers between devices, shards(): recv = lax.ppermute(sent, 'passage', swap)  6.44 us
  transfers between devices with their start and end apart: 8, of which 6 were waited for; matrix products, arithmetic and copies ran while one was open for 3% of the time, Pallas kernels for 1%

profile of v1, /device:TPU:1, one launch (start us, length us, event | category | flops | bytes accessed | tf_op | source)
XLA Modules:
  0.0 146.9 jit_solution(16886309645065731593)
XLA Ops:
  0.7 1.9 %copy-done = bf16[2,2,200,2048]{3,2,1,0:T(8,128)(2,1)S(1)} copy-done((bf16[2,2,200,2048]{3,2,1,0:T(8,128)(2,1)S(1)}, bf16[2,2,200,2048]{3,2,1,0:T(8,128)(2,1)}, u32[]{:S(2)}) %copy-start) | copy-done | bytes 3276824
  2.6 1.9 %copy-done.2 = bf16[2,2,200,2048]{3,2,1,0:T(8,128)(2,1)S(1)} copy-done((bf16[2,2,200,2048]{3,2,1,0:T(8,128)(2,1)S(1)}, bf16[2,2,200,2048]{3,2,1,0:T(8,128)(2,1)}, u32[]{:S(2)}) %copy-start.2) | copy-done | bytes 3276824
  4.5 1.0 copy-done.5
  5.5 2.6 %shard_map.114 = bf16[4,448,1024]{2,1,0:T(8,128)(2,1)} custom-call(s32[1]{0:T(128)} %bitcast.core, bf16[2,2,200,2048]{3,2,1,0:T(8,128)(2,1)S(1)} %copy-done, bf16[2,2,200,2048]{3,2,1,0:T(8,128)(2,1)S(1)} %copy-done.2, bf16[2,2,32,2048]{3,2,1,0:T(8,128)(2,1)S(1)} %copy-done.5), custom_call_target="tpu_custom_call" | custom-call | tf_op jit(solution)/shard_map/pallas_call | solution.py:297
  8.1 3.2 %collective-permute-start.2 = (bf16[4,448,1024]{2,1,0:T(8,128)(2,1)}, bf16[4,448,1024]{2,1,0:T(8,128)(2,1)}, u32[]{:S(2)}, u32[]{:S(2)}) collective-permute-start(bf16[4,448,1024]{2,1,0:T(8,128)(2,1)} %shard_map.114), channel_id=1, source_target_pairs={{0,1},{1,0},{2,3},{3,2},{4,5},{5,4},{6,7},{7,6},{8,9},{9,8},{10,11... | collective-permute-start | bytes 11010056 | tf_op jit(solution)/shard_map/ppermute | solution.py:312
  11.5 6.4 %collective-permute-done.1.recv_ref = bf16[80,3072]{1,0:T(8,128)(2,1)S(1)} collective-permute-done((bf16[80,3072]{1,0:T(8,128)(2,1)S(1)}, bf16[80,3072]{1,0:T(8,128)(2,1)S(1)}, u32[]{:S(2)}, u32[]{:S(2)}) %collective-permute-start.1) | collective-permute-done | bytes 491552 | tf_op jit(solution)/shard_map/ppermute | solution.py:293
  19.2 20.4 %all_to_all.25.part_ref = f32[32,56,128]{2,1,0:T(8,128)S(1)} all-to-all(f32[32,56,128]{2,1,0:T(8,128)S(1)} %get-tuple-element.21), channel_id=1, replica_groups={{0,2,4,6,8,10,12,14,16,18,20,22,24,26,28,30,32,34,36,38,40,42,44,46,48,..., dimensions={0} | all-to-all | bytes 1835008 | tf_op jit(solution)/shard_map/all_to_all | solution.py:287
  41.2 5.6 %all-to-all-start.1 = ((bf16[32,48,128]{2,1,0:T(8,128)(2,1)}), bf16[32,48,128]{2,1,0:T(8,128)(2,1)}, u32[]{:S(2)}, u32[]{:S(2)}) async-start(bf16[32,48,128]{2,1,0:T(8,128)(2,1)} %copy-done.9), calls=%async_computation.1 | async-start | bytes 786432 | tf_op jit(solution)/shard_map/all_to_all | solution.py:287
  48.2 1.4 collective-permute-start
  51.0 4.5 %all-to-all-done.1.qkv_ref = bf16[32,48,128]{2,1,0:T(8,128)(2,1)} async-done(((bf16[32,48,128]{2,1,0:T(8,128)(2,1)}), bf16[32,48,128]{2,1,0:T(8,128)(2,1)}, u32[]{:S(2)}, u32[]{:S(2)}) %all-to-all-start.1) | async-done | bytes 393248 | tf_op jit(solution)/shard_map/all_to_all | solution.py:287
  55.6 1.9 %copy-done.3 = bf16[2,2,200,2048]{3,2,1,0:T(8,128)(2,1)S(1)} copy-done((bf16[2,2,200,2048]{3,2,1,0:T(8,128)(2,1)S(1)}, bf16[2,2,200,2048]{3,2,1,0:T(8,128)(2,1)}, u32[]{:S(2)}) %copy-start.3) | copy-done | bytes 3276824
  57.5 1.0 copy-done.6
  59.9 19.2 %shard_map.115 = (bf16[4,32,1024]{2,1,0:T(8,128)(2,1)S(1)}, bf16[4,32,1024]{2,1,0:T(8,128)(2,1)S(1)}, f32[32,48,128]{2,1,0:T(8,128)S(1)}) custom-call(s32[9]{0:T(128)S(1)} %copy-done.19, s32[8]{0:T(128)S(1)} %copy-done.23, bf16[32,48,128]{2,1,0:T(8,128)(2,1)} %all-to-all-done.1.qkv_ref, bf16[2,2,200,2048]{3,2,1,0:T(8,128)(2,1)S(1)} %copy-done.1, ...), custom_call_target="tpu_custom_call" | custom-call | tf_op jit(solution)/shard_map/pallas_call | solution.py:333
  79.8 15.5 %all_to_all.26.recv_ref = f32[32,48,128]{2,1,0:T(8,128)S(1)} all-to-all(f32[32,48,128]{2,1,0:T(8,128)S(1)} %get-tuple-element.25), channel_id=1, replica_groups={{0,2,4,6,8,10,12,14,16,18,20,22,24,26,28,30,32,34,36,38,40,42,44,46,48,..., dimensions={0} | all-to-all | bytes 1572864 | tf_op jit(solution)/shard_map/all_to_all | solution.py:287
  95.4 14.4 %all_to_all.27.recv_ref.groups_ref = bf16[4,112,128]{2,1,0:T(8,128)(2,1)S(1)} all-to-all(bf16[4,112,128]{2,1,0:T(8,128)(2,1)S(1)} %get-tuple-element.29), channel_id=1, replica_groups=mesh['dp'=4,'passage'=64] {'dp'}, dimensions={0} | all-to-all | bytes 229376 | tf_op jit(solution)/shard_map/all_to_all | solution.py:377
  109.8 1.4 shard_map.117
  111.2 5.1 %all-to-all-start.4 = ((bf16[32,208,128]{2,1,0:T(8,128)(2,1)}), bf16[32,208,128]{2,1,0:T(8,128)(2,1)S(1)}, u32[]{:S(2)}, u32[]{:S(2)}) async-start(bf16[32,208,128]{2,1,0:T(8,128)(2,1)} %shard_map.117), calls=%async_computation.4 | async-start | bytes 3407872 | tf_op jit(solution)/shard_map/all_to_all | solution.py:287
  116.3 4.9 %collective-permute-start.3 = (bf16[4,32,1024]{2,1,0:T(8,128)(2,1)S(1)}, bf16[4,32,1024]{2,1,0:T(8,128)(2,1)S(1)}, u32[]{:S(2)}, u32[]{:S(2)}) collective-permute-start(bf16[4,32,1024]{2,1,0:T(8,128)(2,1)S(1)} %copy-done.25), channel_id=1, source_target_pairs={{0,1},{1,0},{2,3},{3,2},{4,5},{5,4},{6,7},{7,6},{8,9},{9,8},{10,11... | collective-permute-start | bytes 786440 | tf_op jit(solution)/shard_map/ppermute | solution.py:365
  121.2 1.2 collective-permute-done.3
  124.9 9.6 %all-to-all-done.4.recv_ref = bf16[32,208,128]{2,1,0:T(8,128)(2,1)S(1)} async-done(((bf16[32,208,128]{2,1,0:T(8,128)(2,1)}), bf16[32,208,128]{2,1,0:T(8,128)(2,1)S(1)}, u32[]{:S(2)}, u32[]{:S(2)}) %all-to-all-start.4) | async-done | bytes 1703968 | tf_op jit(solution)/shard_map/all_to_all | solution.py:287
  134.5 1.0 shard_map.118
  135.5 6.9 %collective-permute-start.5 = (bf16[64,3072]{1,0:T(8,128)(2,1)S(1)}, bf16[64,3072]{1,0:T(8,128)(2,1)S(1)}, u32[]{:S(2)}, u32[]{:S(2)}) collective-permute-start(bf16[64,3072]{1,0:T(8,128)(2,1)S(1)} %get-tuple-element.37), channel_id=1, source_target_pairs={{0,1},{1,0},{2,3},{3,2},{4,5},{5,4},{6,7},{7,6},{8,9},{9,8},{10,11... | collective-permute-start | bytes 1179656 | tf_op jit(solution)/shard_map/ppermute | solution.py:386
  142.6 1.3 collective-permute-done.4.recv_ref
  144.6 2.4 %shard_map.120 = f32[64,6144]{1,0:T(8,128)} custom-call(s32[1]{0:T(128)} %bitcast.core, f32[64,3072]{1,0:T(8,128)S(1)} %get-tuple-element.36.own_ref, bf16[64,3072]{1,0:T(8,128)(2,1)S(1)} %collective-permute-done.5.recv_ref), custom_call_target="tpu_custom_call" | custom-call | tf_op jit(solution)/shard_map/pallas_call | solution.py:392
  (74 shorter events, 11.3 us)
Async XLA Ops:
  5.5 5.8 %copy-start.4 = (bf16[64,6144]{1,0:T(8,128)(2,1)S(1)}, bf16[64,6144]{1,0:T(8,128)(2,1)}, u32[]{:S(2)}) copy-start(bf16[64,6144]{1,0:T(8,128)(2,1)} %w_ref.3) | copy-start | bytes 2359300
  5.5 5.8 %copy-start.10 = (bf16[2,32,64]{2,1,0:T(8,128)(2,1)S(1)}, bf16[2,32,64]{2,1,0:T(8,128)(2,1)}, u32[]{:S(2)}) copy-start(bf16[2,32,64]{2,1,0:T(8,128)(2,1)} %param.8) | copy-start | bytes 24580
  5.5 5.8 %copy-start.17 = (bf16[64]{0:T(256)(128)(2,1)S(1)}, bf16[64]{0:T(256)(128)(2,1)}, u32[]{:S(2)}) copy-start(bf16[64]{0:T(256)(128)(2,1)} %param.9) | copy-start | bytes 388
  8.1 39.2 %copy-start.27 = (s32[2,1,2]{2,1,0:T(1,128)S(1)}, s32[2,1,2]{2,1,0:T(1,128)}, u32[]{:S(2)}) copy-start(s32[2,1,2]{2,1,0:T(1,128)} %param.14) | copy-start | bytes 52
  8.1 40.0 %copy-start.28 = (s32[2,2]{1,0:T(2,128)S(1)}, s32[2,2]{1,0:T(2,128)}, u32[]{:S(2)}) copy-start(s32[2,2]{1,0:T(2,128)} %param.13) | copy-start | bytes 52
  8.1 47.4 %copy-start.1 = (bf16[2,2,200,2048]{3,2,1,0:T(8,128)(2,1)S(1)}, bf16[2,2,200,2048]{3,2,1,0:T(8,128)(2,1)}, u32[]{:S(2)}) copy-start(bf16[2,2,200,2048]{3,2,1,0:T(8,128)(2,1)} %keys_ref.3) | copy-start | bytes 9830404
  8.1 47.4 %collective-permute-start.2 = (bf16[4,448,1024]{2,1,0:T(8,128)(2,1)}, bf16[4,448,1024]{2,1,0:T(8,128)(2,1)}, u32[]{:S(2)}, u32[]{:S(2)}) collective-permute-start(bf16[4,448,1024]{2,1,0:T(8,128)(2,1)} %shard_map.114), channel_id=1, source_target_pairs={{0,1},{1,0},{2,3},{3,2},{4,5},{5,4},{6,7},{7,6},{8,9},{9,8},{10,11... | collective-permute-start | bytes 11010056 | tf_op jit(solution)/shard_map/ppermute | solution.py:312
  11.4 6.6 %collective-permute-start.1 = (bf16[80,3072]{1,0:T(8,128)(2,1)S(1)}, bf16[80,3072]{1,0:T(8,128)(2,1)S(1)}, u32[]{:S(2)}, u32[]{:S(2)}) collective-permute-start(bf16[80,3072]{1,0:T(8,128)(2,1)S(1)} %shard_map.111), channel_id=1, source_target_pairs={{0,1},{1,0},{2,3},{3,2},{4,5},{5,4},{6,7},{7,6},{8,9},{9,8},{10,11... | collective-permute-start | bytes 1474568 | tf_op jit(solution)/shard_map/ppermute | solution.py:293
  19.2 20.7 %copy-start.13 = (bf16[64,128]{1,0:T(8,128)(2,1)}, bf16[64,128]{1,0:T(8,128)(2,1)S(1)}, u32[]{:S(2)}) copy-start(bf16[64,128]{1,0:T(8,128)(2,1)S(1)} %get-tuple-element.28.pair_ref) | copy-start | bytes 49156
  19.2 20.7 %copy-start.20 = (f32[1,128]{1,0:T(1,128)}, f32[1,128]{1,0:T(1,128)S(1)}, u32[]{:S(2)}) copy-start(f32[1,128]{1,0:T(1,128)S(1)} %get-tuple-element.31.gains_ref) | copy-start | bytes 1540
  41.2 14.3 %copy-start.15 = (f32[16,128]{1,0:T(8,128)}, f32[16,128]{1,0:T(8,128)S(1)}, u32[]{:S(2)}) copy-start(f32[16,128]{1,0:T(8,128)S(1)} %get-tuple-element.27.rate_ref) | copy-start | bytes 24580
  41.2 14.3 %all-to-all-start.1 = ((bf16[32,48,128]{2,1,0:T(8,128)(2,1)}), bf16[32,48,128]{2,1,0:T(8,128)(2,1)}, u32[]{:S(2)}, u32[]{:S(2)}) async-start(bf16[32,48,128]{2,1,0:T(8,128)(2,1)} %copy-done.9), calls=%async_computation.1 | async-start | bytes 786432 | tf_op jit(solution)/shard_map/all_to_all | solution.py:287
  48.2 2.2 %collective-permute-start = (s32[8]{0:T(128)S(1)}, s32[8]{0:T(128)S(1)}, u32[]{:S(2)}, u32[]{:S(2)}) collective-permute-start(s32[8]{0:T(128)S(1)} %pad_add_fusion.1), channel_id=1, source_target_pairs={{0,1},{1,0},{2,3},{3,2},{4,5},{5,4},{6,7},{7,6},{8,9},{9,8},{10,11... | collective-permute-start | bytes 104 | tf_op jit(solution)/shard_map/ppermute | solution.py:296
  59.8 35.4 %copy-start.12 = (f32[48,128]{1,0:T(8,128)S(1)}, f32[48,128]{1,0:T(8,128)}, u32[]{:S(2)}) copy-start(f32[48,128]{1,0:T(8,128)} %copy-done.11) | copy-start | bytes 73732
  59.8 35.4 %copy-start.14 = (bf16[64,128]{1,0:T(8,128)(2,1)S(1)}, bf16[64,128]{1,0:T(8,128)(2,1)}, u32[]{:S(2)}) copy-start(bf16[64,128]{1,0:T(8,128)(2,1)} %copy-done.13) | copy-start | bytes 49156
  59.8 35.4 %copy-start.16 = (f32[16,128]{1,0:T(8,128)S(1)}, f32[16,128]{1,0:T(8,128)}, u32[]{:S(2)}) copy-start(f32[16,128]{1,0:T(8,128)} %copy-done.15) | copy-start | bytes 24580
  95.2 21.1 %copy-start.25 = (bf16[4,32,1024]{2,1,0:T(8,128)(2,1)S(1)}, bf16[4,32,1024]{2,1,0:T(8,128)(2,1)}, u32[]{:S(2)}) copy-start(bf16[4,32,1024]{2,1,0:T(8,128)(2,1)} %copy-done.24) | copy-start | bytes 786436
  109.8 24.7 %copy-start.8 = (bf16[128,3072]{1,0:T(8,128)(2,1)S(1)}, bf16[128,3072]{1,0:T(8,128)(2,1)}, u32[]{:S(2)}) copy-start(bf16[128,3072]{1,0:T(8,128)(2,1)} %copy-done.7) | copy-start | bytes 2359300
  109.8 24.7 %copy-start.21 = (f32[1,128]{1,0:T(1,128)S(1)}, f32[1,128]{1,0:T(1,128)}, u32[]{:S(2)}) copy-start(f32[1,128]{1,0:T(1,128)} %copy-done.20) | copy-start | bytes 1540
  111.2 23.3 %all-to-all-start.4 = ((bf16[32,208,128]{2,1,0:T(8,128)(2,1)}), bf16[32,208,128]{2,1,0:T(8,128)(2,1)S(1)}, u32[]{:S(2)}, u32[]{:S(2)}) async-start(bf16[32,208,128]{2,1,0:T(8,128)(2,1)} %shard_map.117), calls=%async_computation.4 | async-start | bytes 3407872 | tf_op jit(solution)/shard_map/all_to_all | solution.py:287
  116.3 27.5 %copy-start.18 = (bf16[64]{0:T(256)(128)(2,1)S(1)}, bf16[64]{0:T(256)(128)(2,1)}, u32[]{:S(2)}) copy-start(bf16[64]{0:T(256)(128)(2,1)} %param.9) | copy-start | bytes 388
  116.3 6.1 %collective-permute-start.3 = (bf16[4,32,1024]{2,1,0:T(8,128)(2,1)S(1)}, bf16[4,32,1024]{2,1,0:T(8,128)(2,1)S(1)}, u32[]{:S(2)}, u32[]{:S(2)}) collective-permute-start(bf16[4,32,1024]{2,1,0:T(8,128)(2,1)S(1)} %copy-done.25), channel_id=1, source_target_pairs={{0,1},{1,0},{2,3},{3,2},{4,5},{5,4},{6,7},{7,6},{8,9},{9,8},{10,11... | collective-permute-start | bytes 786440 | tf_op jit(solution)/shard_map/ppermute | solution.py:365
  135.5 9.1 %collective-permute-start.5 = (bf16[64,3072]{1,0:T(8,128)(2,1)S(1)}, bf16[64,3072]{1,0:T(8,128)(2,1)S(1)}, u32[]{:S(2)}, u32[]{:S(2)}) collective-permute-start(bf16[64,3072]{1,0:T(8,128)(2,1)S(1)} %get-tuple-element.37), channel_id=1, source_target_pairs={{0,1},{1,0},{2,3},{3,2},{4,5},{5,4},{6,7},{7,6},{8,9},{9,8},{10,11... | collective-permute-start | bytes 1179656 | tf_op jit(solution)/shard_map/ppermute | solution.py:386
  142.5 1.4 collective-permute-start.4
  (13 other events, 13.4 us)

commit v2 on v1

v2 whole, which is shorter than its diff:
```python
import functools

import jax
import jax.numpy as jnp
from jax import lax
from jax.experimental import pallas as pl
from jax.experimental.pallas import tpu as pltpu
from jax.sharding import PartitionSpec as P

D = 4096
EPS = 1e-06
QLEN = 32
ROWS = 64
FEATS = 64
MEM = 200
HALF = 1024
COLS = 3 * HALF
CHIPS = 32
COL_BLOCKS = 8
CHUNK = 48
K_AT, V_AT, PACKED = 32, 240, 448
FOLD = 0.125

BF16 = jnp.bfloat16
F32 = jnp.float32
VMEM = pl.BlockSpec(memory_space=pltpu.VMEM)
SMEM = pl.BlockSpec(memory_space=pltpu.SMEM)
PARAMS = pltpu.CompilerParams(vmem_limit_bytes=24 * 1024 * 1024)
WIDE = pltpu.CompilerParams(vmem_limit_bytes=60 * 1024 * 1024)

NT = (((1,), (1,)), ((), ()))
TN = (((0,), (0,)), ((), ()))


def dot(a, b, dims=(((1,), (0,)), ((), ()))):
    return lax.dot_general(a, b, dims, preferred_element_type=F32)


def lanes_of(index, width):
    return pl.ds(pl.multiple_of(index * width, width), width)


def pack_w(core, length, owner, w_ref, q_ref, gain_ref, mine_ref, out_ref, info_ref):
    lane = lax.broadcasted_iota(jnp.int32, (16, 128), 1)
    values = jnp.zeros((16, 128), F32)
    for s in range(4):
        for kind, value in enumerate((length[s // 2, s % 2], owner[s // 2, 0, s % 2])):
            info_ref[4 * kind + s] = value
            values = jnp.where(lane == 4 * kind + s, value.astype(F32), values)
    info_ref[8] = core[0]
    for ref, half in ((out_ref, 1 - core[0]), (mine_ref, core[0])):
        for b in range(3):
            ref[0:FEATS, b * HALF : (b + 1) * HALF] = w_ref[:, lanes_of(2 * b + half, HALF)]
        for j in range(4):
            ref[64:80, j * 128 : j * 128 + 64] = q_ref[j * 16 : (j + 1) * 16, :]
        ref[64:80, 512:576] = jnp.broadcast_to(gain_ref[...], (16, FEATS))
        ref[64:80, 640:768] = values.astype(BF16)


def pack_memory(core, keys_ref, values_ref, d_ref, out_ref):
    out_ref[0, 0:QLEN] = d_ref[0, 0]
    out_ref[0, K_AT : K_AT + MEM] = keys_ref[0, 0]
    out_ref[0, V_AT : V_AT + MEM] = values_ref[0, 0]


def unpack(ref):
    question = [ref[64:80, j * 128 : j * 128 + 64].astype(F32) for j in range(4)]
    return jnp.concatenate(question, axis=0), ref[64:80, 512:576].astype(F32)[0:1]


def slots_of(recv_ref, info_ref):
    values = recv_ref[64:80, 640:768].astype(F32)[0:1]
    lane = lax.broadcasted_iota(jnp.int32, (1, 128), 1)
    for i in range(8):
        info_ref[i] = jnp.sum(jnp.where(lane == i, values, 0.0)).astype(jnp.int32)


def project(mine_ref, recv_ref, part_ref, wc_ref, pair_ref, gains_ref):
    question, gain = unpack(mine_ref)
    their_question, their_gain = unpack(recv_ref)
    pair = jnp.concatenate([question, their_question], axis=1)
    gains = jnp.concatenate([gain, their_gain], axis=1)
    pair_ref[...] = pair.astype(BF16)
    gains_ref[...] = gains
    scaled = (pair * gains).astype(BF16)
    wc_ref[0:FEATS, :] = mine_ref[0:FEATS, :]
    wc_ref[FEATS:, :] = recv_ref[0:FEATS, :]
    for cb in range(COL_BLOCKS):
        pre = dot(scaled, wc_ref[:, cb * 384 : (cb + 1) * 384])
        for rb in range(4):
            for t in range(3):
                part_ref[rb * COL_BLOCKS + cb, t * 16 : (t + 1) * 16, :] = pre[
                    rb * 16 : (rb + 1) * 16, t * 128 : (t + 1) * 128
                ]
    squares = jnp.sum(pair * pair, axis=1, keepdims=True)
    low = lax.broadcasted_iota(jnp.int32, (8, 128), 1) < 64
    for rb in range(4):
        tile = jnp.where(
            low, squares[rb * 16 : rb * 16 + 8], squares[rb * 16 + 8 : rb * 16 + 16]
        )
        for cb in range(COL_BLOCKS):
            part_ref[rb * COL_BLOCKS + cb, CHUNK : CHUNK + 8, :] = tile


def normalise(part_ref, qkv_ref, pre_ref, rate_ref):
    total = jnp.sum(part_ref[...], axis=0)
    rates = lax.rsqrt(total[CHUNK:] / D + EPS)
    rate = jnp.concatenate([rates[:, 0:1], rates[:, 64:65]], axis=0)
    rate = jnp.broadcast_to(rate, (16, 128))
    pre = total[:CHUNK]
    pre_ref[...] = pre
    rate_ref[...] = rate
    qkv = (pre * jnp.concatenate([rate] * 3, axis=0)).astype(BF16)
    for k in range(CHIPS):
        qkv_ref[k] = qkv


def attend(
    own, oth, qkv_ref, keys_ref, values_ref, d_ref, packed_ref, ctx_own, ctx_oth, grad_ref,
    rows, mask_q, mask_d, kcat, vcat, query, d_rows, scores, d_prob, prob_b, d_scores, total,
):
    step = pl.program_id(0)

    @pl.when(step == 0)
    def _():
        for k in range(CHIPS):
            rb, cb = divmod(k, COL_BLOCKS)
            for t in range(3):
                at = (cb * 3 + t) * 128
                rows[rb * 16 : (rb + 1) * 16, at : at + 128] = qkv_ref[k, t * 16 : (t + 1) * 16, :]
        total[...] = jnp.zeros_like(total)
        head = lax.broadcasted_iota(jnp.int32, (128, 256), 0) // QLEN
        lane = lax.broadcasted_iota(jnp.int32, (128, 256), 1) // 64
        same = jnp.where(head == lane, 1.0, 0.0)
        mask_d[...] = same.astype(BF16)
        mask_q[...] = (same * FOLD).astype(BF16)
        for unit in range(8):
            kcat[unit, 224:256] = jnp.zeros((32, 256), BF16)
            vcat[unit, 224:256] = jnp.zeros((32, 256), BF16)

    key_at = lax.broadcasted_iota(jnp.int32, (1, 256), 1)
    lane_head = lax.broadcasted_iota(jnp.int32, (QLEN, 256), 1) // 64

    def diagonal(full):
        out = full[0:QLEN]
        for h in range(1, 4):
            out = jnp.where(lane_head == h, full[h * QLEN : (h + 1) * QLEN], out)
        return out

    units = [(side, hg) for side in range(2) for hg in range(4)]
    infos = (own, oth)
    for side, hg in units:
        info = infos[side]
        at = pl.ds(pl.multiple_of(info[4 + step] * QLEN, QLEN), QLEN)
        unit = side * 4 + hg
        lanes = slice(hg * 256, (hg + 1) * 256)
        kc, vc = kcat.at[unit], vcat.at[unit]
        kc[0:QLEN] = rows[at, HALF + hg * 256 : HALF + (hg + 1) * 256]
        vc[0:QLEN] = rows[at, 2 * HALF + hg * 256 : 2 * HALF + (hg + 1) * 256]
        if side == 0:
            kc[QLEN : QLEN + MEM] = keys_ref[0, 0, :, lanes]
            vc[QLEN : QLEN + MEM] = values_ref[0, 0, :, lanes]
            d_out = d_ref[0, 0, :, lanes]
        else:
            kc[QLEN : QLEN + MEM] = packed_ref[0, K_AT : K_AT + MEM, lanes]
            vc[QLEN : QLEN + MEM] = packed_ref[0, V_AT : V_AT + MEM, lanes]
            d_out = packed_ref[0, 0:QLEN, lanes]
        query[unit] = jnp.concatenate([rows[at, lanes]] * 4, axis=0) * mask_q[...]
        d_rows[unit] = jnp.concatenate([d_out] * 4, axis=0) * mask_d[...]
    for side, hg in units:
        unit = side * 4 + hg
        scores[unit] = dot(query[unit], kcat[unit], NT)
        d_prob[unit] = dot(d_rows[unit], vcat[unit], NT)
    for side, hg in units:
        unit = side * 4 + hg
        live = key_at < infos[side][step] + QLEN
        for h in range(4):
            part = slice(h * QLEN, (h + 1) * QLEN)
            score = jnp.where(live, scores[unit, part], -1e30)
            expo = jnp.exp(score - jnp.max(score, axis=1, keepdims=True))
            prob = expo * (1.0 / jnp.sum(expo, axis=1, keepdims=True))
            d_p = d_prob[unit, part]
            inner = jnp.sum(d_p * prob, axis=1, keepdims=True)
            prob_b[unit, part] = prob.astype(BF16)
            d_scores[unit, part] = (prob * (d_p - inner)).astype(BF16)
    for side, hg in units:
        unit = side * 4 + hg
        lanes = slice(hg * 256, (hg + 1) * 256)
        question = infos[side][4 + step]
        context = diagonal(dot(prob_b[unit], vcat[unit])).astype(BF16)
        if side == 0:
            ctx_own[0, :, lanes] = context
        else:
            ctx_oth[0, :, lanes] = context
        grads = (
            diagonal(dot(d_scores[unit], kcat[unit])) * FOLD,
            dot(d_scores[unit, :, 0:QLEN], query[unit], TN),
            dot(prob_b[unit, :, 0:QLEN], d_rows[unit], TN),
        )
        for kind, grad in enumerate(grads):
            for tt in range(2):
                cb, t = divmod(kind * 8 + hg * 2 + tt, 3)
                for r in range(2):
                    k = (2 * question + r) * COL_BLOCKS + cb
                    total[k, t * 16 : (t + 1) * 16, :] += grad[
                        r * 16 : (r + 1) * 16, tt * 128 : (tt + 1) * 128
                    ]

    @pl.when(step == 3)
    def _():
        grad_ref[...] = total[...].astype(BF16)


def join_context(core, own_ref, theirs_ref, out_ref):
    out_ref[:, :, lanes_of(core[0], HALF)] = own_ref[...]
    out_ref[:, :, lanes_of(1 - core[0], HALF)] = theirs_ref[...]


def split_rows(value):
    high = value.astype(BF16).astype(F32)
    low = lax.broadcasted_iota(jnp.int32, value.shape, 1) < 64
    return jnp.where(low, high, value - high).astype(BF16)


def finish_grad(recv_ref, pre_ref, rate_ref, pair_ref, out_ref, cubed_ref):
    grad = jnp.sum(recv_ref[...].astype(F32), axis=0)
    rate = rate_ref[...]
    product = grad * pre_ref[...]
    product = product[0:16] + product[16:32] + product[32:48]
    d_rate = jnp.sum(product, axis=1, keepdims=True)
    cubed_ref[...] = split_rows(d_rate * rate * rate * rate)
    out_ref[0, 0:CHUNK] = (grad * jnp.concatenate([rate] * 3, axis=0)).astype(BF16)
    out_ref[0, CHUNK:] = pair_ref[...]


def spread(first_ref, second_ref, cubed_ref, out_ref):
    for k in range(CHIPS):
        for g in range(4):
            ref = first_ref if g < 2 else second_ref
            out_ref[k, g * CHUNK : (g + 1) * CHUNK] = ref[g % 2, 0:CHUNK]
        out_ref[k, 4 * CHUNK :] = cubed_ref[...]


def weight_grads(
    recv_ref, first_ref, second_ref, gains_ref, wc_ref, send_ref, small_ref, d_pre, scaled, d_in
):
    pairs = [ref[g, CHUNK:] for ref in (first_ref, second_ref) for g in range(2)]
    pairs = jnp.concatenate(pairs, axis=0).astype(F32)
    scaled_t = (pairs * gains_ref[...]).T.astype(BF16)
    scaled[...] = scaled_t[0:FEATS]
    for cb in range(COL_BLOCKS):
        for rb in range(4):
            for g in range(4):
                for t in range(3):
                    d_pre[
                        cb, g * ROWS + rb * 16 : g * ROWS + (rb + 1) * 16, t * 128 : (t + 1) * 128
                    ] = recv_ref[
                        rb * COL_BLOCKS + cb, g * CHUNK + t * 16 : g * CHUNK + (t + 1) * 16, :
                    ]
        block = d_pre[cb]
        at = slice(cb * 384, (cb + 1) * 384)
        send_ref[0:FEATS, at] = dot(scaled_t[FEATS:], block).astype(BF16)
        term = dot(block, wc_ref[:, at], NT)
        if cb == 0:
            d_in[...] = term
        else:
            d_in[...] += term
    cubed = []
    for rb in range(4):
        total = jnp.zeros((16, 128), F32)
        for cb in range(COL_BLOCKS):
            total += recv_ref[rb * COL_BLOCKS + cb, 4 * CHUNK :].astype(F32)
        cubed.append(total[:, 0:1] + total[:, 64:65])
    cubed = jnp.broadcast_to(jnp.concatenate(cubed, axis=0), (ROWS, 128))
    mine = d_in[0:ROWS]
    d_gain = jnp.broadcast_to(jnp.sum(pairs * d_in[...], axis=0, keepdims=True), (16, 128))
    low = lax.broadcasted_iota(jnp.int32, (ROWS, 128), 1) < 64
    small_ref[0:ROWS] = mine
    small_ref[ROWS : 2 * ROWS] = cubed
    small_ref[2 * ROWS :] = d_gain
    for value, at in ((jnp.where(low, cubed, mine), slice(0, 64)), (d_gain, slice(64, 80))):
        high = value.astype(BF16)
        send_ref[at, COLS : COLS + 128] = high
        send_ref[at, COLS + 128 : COLS + 256] = (value - high.astype(F32)).astype(BF16)


def columns_out(half, held, dw_ref, sems):
    return [
        pltpu.make_async_copy(
            held.at[:, pl.ds(b * HALF, HALF)],
            dw_ref.at[:, lanes_of(2 * b + half, HALF)],
            sems.at[b],
        )
        for b in range(3)
    ]


def own_weight(core, d_pre_ref, scaled_ref, dw_ref, held, sems):
    for cb in range(COL_BLOCKS):
        held[:, cb * 384 : (cb + 1) * 384] = dot(scaled_ref[...], d_pre_ref[cb])
    copies = columns_out(core[0], held, dw_ref, sems)
    for copy in copies:
        copy.start()
    for copy in copies:
        copy.wait()


def finish(core, recv_ref, small_ref, mine_ref, in_ref, dq_ref, dg_ref, dw_ref, held, sems):
    copies = columns_out(1 - core[0], held, dw_ref, sems)
    for b in range(3):
        at = slice(b * HALF, (b + 1) * HALF)
        held[:, at] = recv_ref[0:FEATS, at].astype(F32)
        copies[b].start()
    theirs = recv_ref[:, COLS : COLS + 128].astype(F32)
    theirs += recv_ref[:, COLS + 128 : COLS + 256].astype(F32)
    d_input = small_ref[0:ROWS, 0:FEATS] + theirs[0:ROWS, 64:128]
    cubed = small_ref[ROWS : 2 * ROWS, 0:1] + theirs[0:ROWS, 0:1]
    question, gain = unpack(mine_ref)
    dq_ref[...] = (gain * d_input - cubed * question / D).astype(BF16)
    dg_ref[...] = small_ref[2 * ROWS : 2 * ROWS + 1, 0:FEATS] + theirs[ROWS : ROWS + 1, 64:128]
    for copy in copies:
        copy.wait()


def attention(own_info, other_info, qkv, mem_keys, mem_values, d_context, packed):
    return pl.pallas_call(
        attend,
        out_shape=[
            jax.ShapeDtypeStruct((4, QLEN, HALF), BF16),
            jax.ShapeDtypeStruct((4, QLEN, HALF), BF16),
            jax.ShapeDtypeStruct((CHIPS, CHUNK, 128), BF16),
        ],
        grid_spec=pltpu.PrefetchScalarGridSpec(
            num_scalar_prefetch=2,
            grid=(4,),
            in_specs=[
                pl.BlockSpec((CHIPS, CHUNK, 128), lambda s, c, o: (0, 0, 0)),
                pl.BlockSpec((1, 1, MEM, HALF), lambda s, c, o: (s // 2, s % 2, 0, c[8])),
                pl.BlockSpec((1, 1, MEM, HALF), lambda s, c, o: (s // 2, s % 2, 0, c[8])),
                pl.BlockSpec((1, 1, QLEN, HALF), lambda s, c, o: (s // 2, s % 2, 0, c[8])),
                pl.BlockSpec((1, PACKED, HALF), lambda s, c, o: (s, 0, 0)),
            ],
            out_specs=[
                pl.BlockSpec((1, QLEN, HALF), lambda s, c, o: (s, 0, 0)),
                pl.BlockSpec((1, QLEN, HALF), lambda s, c, o: (s, 0, 0)),
                pl.BlockSpec((CHIPS, CHUNK, 128), lambda s, c, o: (0, 0, 0)),
            ],
            scratch_shapes=[
                pltpu.VMEM((ROWS, COLS), BF16),
                pltpu.VMEM((128, 256), BF16),
                pltpu.VMEM((128, 256), BF16),
                pltpu.VMEM((8, 256, 256), BF16),
                pltpu.VMEM((8, 256, 256), BF16),
                pltpu.VMEM((8, 128, 256), BF16),
                pltpu.VMEM((8, 128, 256), BF16),
                pltpu.VMEM((8, 128, 256), F32),
                pltpu.VMEM((8, 128, 256), F32),
                pltpu.VMEM((8, 128, 256), BF16),
                pltpu.VMEM((8, 128, 256), BF16),
                pltpu.VMEM((CHIPS, CHUNK, 128), F32),
            ],
        ),
        compiler_params=WIDE,
    )(own_info, other_info, qkv, mem_keys, mem_values, d_context, packed)


def call(body, outs, specs, scratch=(), scalars=0, params=PARAMS):
    return pl.pallas_call(
        body,
        out_shape=[jax.ShapeDtypeStruct(s, t) for s, t in outs],
        in_specs=specs,
        out_specs=[VMEM] * (len(outs) - scalars) + [SMEM] * scalars,
        scratch_shapes=list(scratch),
        compiler_params=params,
    )


def shards(question, norm_gain, w_qkv, mem_keys, mem_values, mem_length, owner, d_context):
    core = jnp.reshape(lax.axis_index("passage") % 2, (1,)).astype(jnp.int32)
    swap = [(i, i ^ 1) for i in range(2 * CHIPS)]
    same_core = [[c + 2 * i for i in range(CHIPS)] for c in range(2)]

    def exchange(x):
        return lax.all_to_all(x, "passage", 0, 0, tiled=True, axis_index_groups=same_core)

    q64 = question.reshape(ROWS, FEATS)
    gain = norm_gain.reshape(1, FEATS)

    mine, sent, info = call(
        pack_w,
        [((80, COLS), BF16), ((80, COLS), BF16), ((9,), jnp.int32)],
        [SMEM] * 3 + [VMEM] * 3,
        scalars=1,
        params=WIDE,
    )(core, mem_length, owner, w_qkv, q64, gain)
    recv = lax.ppermute(sent, "passage", swap)

    memory_core, _ = lax.optimization_barrier((core, sent))
    half = lambda s, c: (s // 2, s % 2, 0, 1 - c[0])
    packed = pl.pallas_call(
        pack_memory,
        out_shape=jax.ShapeDtypeStruct((4, PACKED, HALF), BF16),
        grid_spec=pltpu.PrefetchScalarGridSpec(
            num_scalar_prefetch=1,
            grid=(4,),
            in_specs=[
                pl.BlockSpec((1, 1, MEM, HALF), half),
                pl.BlockSpec((1, 1, MEM, HALF), half),
                pl.BlockSpec((1, 1, QLEN, HALF), half),
            ],
            out_specs=pl.BlockSpec((1, PACKED, HALF), lambda s, c: (s, 0, 0)),
        ),
        compiler_params=WIDE,
    )(memory_core, mem_keys, mem_values, d_context)
    packed, recv = lax.optimization_barrier((packed, recv))
    packed = lax.ppermute(packed, "passage", swap)

    part, wc, pair, gains = call(
        project,
        [
            ((CHIPS, CHUNK + 8, 128), F32),
            ((2 * FEATS, COLS), BF16),
            ((ROWS, 2 * FEATS), BF16),
            ((1, 2 * FEATS), F32),
        ],
        [VMEM] * 2,
    )(mine, recv)
    (other_info,) = call(slots_of, [((8,), jnp.int32)], [VMEM], scalars=1)(recv)
    part = exchange(part)
    qkv, pre, rate = call(
        normalise,
        [((CHIPS, CHUNK, 128), BF16), ((CHUNK, 128), F32), ((16, 128), F32)],
        [VMEM],
    )(part)
    qkv = exchange(qkv)

    ctx_own, ctx_oth, grads = attention(
        info, other_info, qkv, mem_keys, mem_values, d_context, packed
    )
    ctx_mine = lax.ppermute(ctx_oth, "passage", swap)
    context = pl.pallas_call(
        join_context,
        out_shape=jax.ShapeDtypeStruct((4, QLEN, 2 * HALF), BF16),
        grid_spec=pltpu.PrefetchScalarGridSpec(
            num_scalar_prefetch=1,
            grid=(2,),
            in_specs=[pl.BlockSpec((2, QLEN, HALF), lambda s, c: (s, 0, 0))] * 2,
            out_specs=pl.BlockSpec((2, QLEN, 2 * HALF), lambda s, c: (s, 0, 0)),
        ),
        compiler_params=PARAMS,
    )(core, ctx_own, ctx_mine)

    grads = exchange(grads)
    chunk, cubed = call(
        finish_grad,
        [((1, CHUNK + ROWS, 128), BF16), ((16, 128), BF16)],
        [VMEM] * 4,
    )(grads, pre, rate, pair)
    first = jnp.concatenate([chunk, lax.ppermute(chunk, "dp", [(g, g ^ 1) for g in range(4)])])
    second = lax.ppermute(first, "dp", [(g, g ^ 3) for g in range(4)])
    (d_pre,) = call(spread, [((CHIPS, 4 * CHUNK + 16, 128), BF16)], [VMEM] * 3)(
        first, second, cubed
    )
    d_pre, context = lax.optimization_barrier((exchange(d_pre), context))
    send, small, blocks, scaled = call(
        weight_grads,
        [
            ((80, COLS + 256), BF16),
            ((2 * ROWS + 16, 128), F32),
            ((COL_BLOCKS, 4 * ROWS, 384), BF16),
            ((FEATS, 4 * ROWS), BF16),
        ],
        [VMEM] * 5,
        [pltpu.VMEM((4 * ROWS, 128), F32)],
    )(d_pre, first, second, gains, wc)
    recv = lax.ppermute(send, "passage", swap)
    any_space = pl.BlockSpec(memory_space=pl.ANY)
    staging = [pltpu.VMEM((FEATS, COLS), F32), pltpu.SemaphoreType.DMA((3,))]
    d_weight = pl.pallas_call(
        own_weight,
        out_shape=jax.ShapeDtypeStruct((FEATS, 2 * COLS), F32),
        in_specs=[SMEM, VMEM, VMEM],
        out_specs=any_space,
        scratch_shapes=staging,
        compiler_params=PARAMS,
    )(core, blocks, scaled)
    d_question, d_gain, d_weight = pl.pallas_call(
        finish,
        out_shape=[
            jax.ShapeDtypeStruct((ROWS, FEATS), BF16),
            jax.ShapeDtypeStruct((1, FEATS), F32),
            jax.ShapeDtypeStruct((FEATS, 2 * COLS), F32),
        ],
        in_specs=[SMEM] + [VMEM] * 3 + [any_space],
        out_specs=[VMEM, VMEM, any_space],
        scratch_shapes=staging,
        input_output_aliases={4: 2},
        compiler_params=PARAMS,
    )(core, recv, small, mine, d_weight)
    return (
        context.reshape(2, 2, QLEN, 2 * HALF),
        d_question.reshape(question.shape),
        d_gain.reshape(norm_gain.shape),
        d_weight,
    )


def solution(mesh):
    return jax.shard_map(
        shards,
        mesh=mesh,
        in_specs=(
            P("dp", None, "passage"),
            P("passage"),
            P("passage", None),
            P("passage", "dp", None, None),
            P("passage", "dp", None, None),
            P("passage", "dp"),
            P("passage", "dp", None),
            P("passage", "dp", None, None),
        ),
        out_specs=(
            P("passage", "dp", None, None),
            P("dp", None, "passage"),
            P("passage"),
            P("passage", None),
        ),
        check_vma=False,
    )
```

time: 148 us -> 115 us (0.78)
  blocking collectives: 50.3 us -> 32.9 us
  local copies, waits for them, and re-layouts: 14.1 us -> 0.77 us
  starting transfers between devices: 27.4 us -> 33.9 us
  other arithmetic: 3.15 us -> 0 us
  Pallas kernels: 28 us -> 25.1 us
  waiting for transfers between devices: 23.2 us -> 21.5 us
    all_to_all x1 -> x0, blocking collectives: 14.4 us -> none  [shards(): groups = lax.all_to_all(chunk, 'dp', 0, 0, tiled=True)]
    unnamed x59 -> x9, local copies, waits for them, and re-layouts: 13.9 us -> 0.76 us
    ppermute x3, starting transfers between devices: 8.44 us -> 15 us  [the longest x1 7.45 us: shards(): recv = lax.ppermute(send, 'passage', swap)]
    ppermute x1, waiting for transfers between devices: 6.44 us -> 0.01 us  [shards(): recv = lax.ppermute(sent, 'passage', swap)]
    pallas_call x7 -> x9, Pallas kernels: 24.9 us -> 19.5 us  [the longest x1 10.4 us: attention(): pl.pallas_call(attend, out_shape=[jax.ShapeDtypeStruct((4, QLEN, HALF), B...]
    ppermute x1, starting transfers between devices: 0.12 us -> 3.33 us  [shards(): recv = lax.ppermute(sent, 'passage', swap)]
    ppermute x1, starting transfers between devices: 3.24 us -> 0.05 us  [shards(): packed = lax.ppermute(packed, 'passage', swap)]
    all_to_all x2, blocking collectives: 35.9 us -> 32.9 us  [exchange(): lax.all_to_all(x, 'passage', 0, 0, tiled=True, axis_index_groups=same_core)]
  transfers between devices with their start and end apart: 8 -> 8, of which waited for: 6 -> 6; matrix products, arithmetic and copies ran while one was open for 3% -> 0% of each run, Pallas kernels for 1% -> 7%
where the time goes in v2:
time: 115 us
  starting transfers between devices  33.9 us (29%)
  blocking collectives  32.9 us (29%)
  Pallas kernels  25.1 us (22%)
  waiting for transfers between devices  21.5 us (19%)
    all_to_all x2, blocking collectives, exchange(): lax.all_to_all(x, 'passage', 0, 0, tiled=True, axis_index_groups=same_core)  32.9 us
    all_to_all x2, waiting for transfers between devices, exchange(): lax.all_to_all(x, 'passage', 0, 0, tiled=True, axis_index_groups=same_core)  16.9 us
    pallas_call x1, Pallas kernels, attention(): pl.pallas_call(attend, out_shape=[jax.ShapeDtypeStruct((4, QLEN, HALF), B...  10.4 us
    all_to_all x2, starting transfers between devices, exchange(): lax.all_to_all(x, 'passage', 0, 0, tiled=True, axis_index_groups=same_core)  9.64 us
    ppermute x1, starting transfers between devices, shards(): recv = lax.ppermute(send, 'passage', swap)  7.45 us
    ppermute x1, starting transfers between devices, shards(): ctx_mine = lax.ppermute(ctx_oth, 'passage', swap)  5.95 us
    ppermute x1, starting transfers between devices, shards(): second = lax.ppermute(first, 'dp', [(g, g ^ 3) for g in range(4)])  4.5 us
    pallas_call x1, Pallas kernels, shards(): pl.pallas_call(pack_memory, out_shape=jax.ShapeDtypeStruct((4, PACKED, HA...  4.32 us
  transfers between devices with their start and end apart: 8, of which 6 were waited for; matrix products, arithmetic and copies ran while one was open for 0% of the time, Pallas kernels for 7%

profile of v2, /device:TPU:1, one launch (start us, length us, event | category | flops | bytes accessed | tf_op | source)
XLA Modules:
  0.0 114.9 jit_solution(9047445684657269729)
XLA Ops:
  0.6 2.2 %shard_map.111 = (bf16[80,3072]{1,0:T(8,128)(2,1)}, bf16[80,3072]{1,0:T(8,128)(2,1)}, s32[9]{0:T(128)}) custom-call(s32[1]{0:T(128)} %bitcast.core, s32[2,2]{1,0:T(2,128)} %length.1, s32[2,1,2]{2,1,0:T(1,128)} %owner.1, bf16[64,6144]{1,0:T(8,128)(2,1)} %w_ref.1, bf16[64,64]{1,0:T(8,128)(2,1)} %bitcast.7, bf16[1,64]{1,0:T(2,128)(2,1)} %bitcast.8), custom_call_target="tpu_custom_call" | custom-call | tf_op jit(solution)/shard_map/pallas_call | solution.py:389
  2.8 3.3 %collective-permute-start = (bf16[80,3072]{1,0:T(8,128)(2,1)}, bf16[80,3072]{1,0:T(8,128)(2,1)S(1)}, u32[]{:S(2)}, u32[]{:S(2)}) collective-permute-start(bf16[80,3072]{1,0:T(8,128)(2,1)} %get-tuple-element.32), channel_id=1, source_target_pairs={{0,1},{1,0},{2,3},{3,2},{4,5},{5,4},{6,7},{7,6},{8,9},{9,8},{10,11... | collective-permute-start | bytes 1474568 | tf_op jit(solution)/shard_map/ppermute | solution.py:396
  6.2 4.3 %shard_map.112 = bf16[4,448,1024]{2,1,0:T(8,128)(2,1)} custom-call(s32[1]{0:T(128)} %bitcast.core, bf16[2,2,200,2048]{3,2,1,0:T(8,128)(2,1)} %keys_ref.3, bf16[2,2,200,2048]{3,2,1,0:T(8,128)(2,1)} %values_ref.3, bf16[2,2,32,2048]{3,2,1,0:T(8,128)(2,1)} %d_ref.3), custom_call_target="tpu_custom_call" | custom-call | tf_op jit(solution)/shard_map/pallas_call | solution.py:400
  10.9 20.2 %all_to_all.20.part_ref = f32[32,56,128]{2,1,0:T(8,128)S(1)} all-to-all(f32[32,56,128]{2,1,0:T(8,128)S(1)} %get-tuple-element.36), channel_id=1, replica_groups={{0,2,4,6,8,10,12,14,16,18,20,22,24,26,28,30,32,34,36,38,40,42,44,46,48,..., dimensions={0} | all-to-all | bytes 1835008 | tf_op jit(solution)/shard_map/all_to_all | solution.py:384
  31.1 0.9 shard_map.115
  32.1 5.4 %all-to-all-start.1 = ((bf16[32,48,128]{2,1,0:T(8,128)(2,1)}), bf16[32,48,128]{2,1,0:T(8,128)(2,1)S(1)}, u32[]{:S(2)}, u32[]{:S(2)}) async-start(bf16[32,48,128]{2,1,0:T(8,128)(2,1)} %get-tuple-element.37), calls=%async_computation.1 | async-start | bytes 786432 | tf_op jit(solution)/shard_map/all_to_all | solution.py:384
  38.2 7.9 %all-to-all-done.1.qkv_ref = bf16[32,48,128]{2,1,0:T(8,128)(2,1)S(1)} async-done(((bf16[32,48,128]{2,1,0:T(8,128)(2,1)}), bf16[32,48,128]{2,1,0:T(8,128)(2,1)S(1)}, u32[]{:S(2)}, u32[]{:S(2)}) %all-to-all-start.1) | async-done | bytes 393248 | tf_op jit(solution)/shard_map/all_to_all | solution.py:384
  46.1 0.7 copy-done.3
  46.9 10.4 %shard_map.116 = (bf16[4,32,1024]{2,1,0:T(8,128)(2,1)}, bf16[4,32,1024]{2,1,0:T(8,128)(2,1)}, bf16[32,48,128]{2,1,0:T(8,128)(2,1)}) custom-call(s32[9]{0:T(128)} %get-tuple-element.31.own, s32[8]{0:T(128)} %copy-done.2, bf16[32,48,128]{2,1,0:T(8,128)(2,1)} %copy-done.3, bf16[2,2,200,2048]{3,2,1,0:T(8,128)(2,1)} %keys_ref.3, ...), custom_call_target="tpu_custom_call" | custom-call | tf_op jit(solution)/shard_map/pallas_call | solution.py:326
  57.3 12.7 %all_to_all.21.recv_ref = bf16[32,48,128]{2,1,0:T(8,128)(2,1)S(1)} all-to-all(bf16[32,48,128]{2,1,0:T(8,128)(2,1)} %get-tuple-element.39), channel_id=1, replica_groups={{0,2,4,6,8,10,12,14,16,18,20,22,24,26,28,30,32,34,36,38,40,42,44,46,48,..., dimensions={0} | all-to-all | bytes 786432 | tf_op jit(solution)/shard_map/all_to_all | solution.py:384
  70.2 3.0 %collective-permute-start.2 = (bf16[1,112,128]{2,1,0:T(8,128)(2,1)S(1)}, bf16[1,112,128]{2,1,0:T(8,128)(2,1)S(1)}, u32[]{:S(2)}, u32[]{:S(2)}) collective-permute-start(bf16[1,112,128]{2,1,0:T(8,128)(2,1)S(1)} %get-tuple-element.43), channel_id=1, source_target_pairs={{0,64},{64,0},{128,192},{192,128},{1,65},{65,1},{129,193},{193,129... | collective-permute-start | bytes 86024 | tf_op jit(solution)/shard_map/ppermute | solution.py:459
  73.2 1.3 %collective-permute-done.2 = bf16[1,112,128]{2,1,0:T(8,128)(2,1)S(1)} collective-permute-done((bf16[1,112,128]{2,1,0:T(8,128)(2,1)S(1)}, bf16[1,112,128]{2,1,0:T(8,128)(2,1)S(1)}, u32[]{:S(2)}, u32[]{:S(2)}) %collective-permute-start.2) | collective-permute-done | bytes 28704 | tf_op jit(solution)/shard_map/ppermute | solution.py:459
  74.5 4.5 %collective-permute-start.3 = (bf16[2,112,128]{2,1,0:T(8,128)(2,1)S(1)}, bf16[2,112,128]{2,1,0:T(8,128)(2,1)S(1)}, u32[]{:S(2)}, u32[]{:S(2)}) collective-permute-start(bf16[2,112,128]{2,1,0:T(8,128)(2,1)S(1)} %constant_dynamic-update-slice_fusion.first_ref), channel_id=1, source_target_pairs={{0,192},{64,128},{128,64},{192,0},{1,193},{65,129},{129,65},{193,1... | collective-permute-start | bytes 172040 | tf_op jit(solution)/shard_map/ppermute | solution.py:460
  79.0 1.7 %collective-permute-done.3.second_ref = bf16[2,112,128]{2,1,0:T(8,128)(2,1)S(1)} collective-permute-done((bf16[2,112,128]{2,1,0:T(8,128)(2,1)S(1)}, bf16[2,112,128]{2,1,0:T(8,128)(2,1)S(1)}, u32[]{:S(2)}, u32[]{:S(2)}) %collective-permute-start.3) | collective-permute-done | bytes 57376 | tf_op jit(solution)/shard_map/ppermute | solution.py:460
  80.6 1.4 %shard_map.118 = bf16[32,208,128]{2,1,0:T(8,128)(2,1)} custom-call(bf16[2,112,128]{2,1,0:T(8,128)(2,1)S(1)} %constant_dynamic-update-slice_fusion.first_ref, bf16[2,112,128]{2,1,0:T(8,128)(2,1)S(1)} %collective-permute-done.3.second_ref, bf16[16,128]{1,0:T(8,128)(2,1)S(1)} %get-tuple-element.44.cubed_ref), custom_call_target="tpu_custom_call" | custom-call | tf_op jit(solution)/shard_map/pallas_call | solution.py:461
  82.1 4.2 %all-to-all-start.3 = ((bf16[32,208,128]{2,1,0:T(8,128)(2,1)}), bf16[32,208,128]{2,1,0:T(8,128)(2,1)S(1)}, u32[]{:S(2)}, u32[]{:S(2)}) async-start(bf16[32,208,128]{2,1,0:T(8,128)(2,1)} %shard_map.118), calls=%async_computation.3 | async-start | bytes 3407872 | tf_op jit(solution)/shard_map/all_to_all | solution.py:384
  86.3 6.0 %collective-permute-start.4 = (bf16[4,32,1024]{2,1,0:T(8,128)(2,1)}, bf16[4,32,1024]{2,1,0:T(8,128)(2,1)S(1)}, u32[]{:S(2)}, u32[]{:S(2)}) collective-permute-start(bf16[4,32,1024]{2,1,0:T(8,128)(2,1)} %get-tuple-element.46), channel_id=1, source_target_pairs={{0,1},{1,0},{2,3},{3,2},{4,5},{5,4},{6,7},{7,6},{8,9},{9,8},{10,11... | collective-permute-start | bytes 786440 | tf_op jit(solution)/shard_map/ppermute | solution.py:440
  92.2 1.4 %collective-permute-done.4.theirs_ref = bf16[4,32,1024]{2,1,0:T(8,128)(2,1)S(1)} collective-permute-done((bf16[4,32,1024]{2,1,0:T(8,128)(2,1)}, bf16[4,32,1024]{2,1,0:T(8,128)(2,1)S(1)}, u32[]{:S(2)}, u32[]{:S(2)}) %collective-permute-start.4) | collective-permute-done | bytes 262176 | tf_op jit(solution)/shard_map/ppermute | solution.py:440
  93.6 0.8 shard_map.119
  94.4 9.0 %all-to-all-done.3.recv_ref = bf16[32,208,128]{2,1,0:T(8,128)(2,1)S(1)} async-done(((bf16[32,208,128]{2,1,0:T(8,128)(2,1)}), bf16[32,208,128]{2,1,0:T(8,128)(2,1)S(1)}, u32[]{:S(2)}, u32[]{:S(2)}) %all-to-all-start.3) | async-done | bytes 1703968 | tf_op jit(solution)/shard_map/all_to_all | solution.py:384
  103.4 1.0 shard_map.120
  104.4 7.4 %collective-permute-start.5 = (bf16[80,3328]{1,0:T(8,128)(2,1)S(1)}, bf16[80,3328]{1,0:T(8,128)(2,1)S(1)}, u32[]{:S(2)}, u32[]{:S(2)}) collective-permute-start(bf16[80,3328]{1,0:T(8,128)(2,1)S(1)} %get-tuple-element.51), channel_id=1, source_target_pairs={{0,1},{1,0},{2,3},{3,2},{4,5},{5,4},{6,7},{7,6},{8,9},{9,8},{10,11... | collective-permute-start | bytes 1597448 | tf_op jit(solution)/shard_map/ppermute | solution.py:476
  111.9 1.2 %shard_map.121.in_ref = f32[64,6144]{1,0:T(8,128)} custom-call(s32[1]{0:T(128)} %bitcast.core, bf16[8,256,384]{2,1,0:T(8,128)(2,1)S(1)} %get-tuple-element.53.d_pre_ref, bf16[64,256]{1,0:T(8,128)(2,1)S(1)} %get-tuple-element.54.scaled_ref), custom_call_target="tpu_custom_call" | custom-call | tf_op jit(solution)/shard_map/pallas_call | solution.py:479
  113.4 1.5 %shard_map.122 = (bf16[64,64]{1,0:T(8,128)(2,1)}, f32[1,64]{1,0:T(1,128)}, f32[64,6144]{1,0:T(8,128)}) custom-call(s32[1]{0:T(128)} %bitcast.core, bf16[80,3328]{1,0:T(8,128)(2,1)S(1)} %collective-permute-done.5.recv_ref, f32[144,128]{1,0:T(8,128)S(1)} %get-tuple-element.52.small_ref, bf16[80,3072]{1,0:T(8,128)(2,1)S(1)} %copy-done, ...), custom_call_target="tpu_custom_call", output_to_operand_aliasing={{2}: (4, {})} | custom-call | tf_op jit(solution)/shard_map/pallas_call | solution.py:487
  (16 shorter events, 1.6 us)
Async XLA Ops:
  2.8 7.7 %copy-start = (bf16[80,3072]{1,0:T(8,128)(2,1)S(1)}, bf16[80,3072]{1,0:T(8,128)(2,1)}, u32[]{:S(2)}) copy-start(bf16[80,3072]{1,0:T(8,128)(2,1)} %get-tuple-element.35.mine_ref) | copy-start | bytes 1474564
  2.8 7.7 %collective-permute-start = (bf16[80,3072]{1,0:T(8,128)(2,1)}, bf16[80,3072]{1,0:T(8,128)(2,1)S(1)}, u32[]{:S(2)}, u32[]{:S(2)}) collective-permute-start(bf16[80,3072]{1,0:T(8,128)(2,1)} %get-tuple-element.32), channel_id=1, source_target_pairs={{0,1},{1,0},{2,3},{3,2},{4,5},{5,4},{6,7},{7,6},{8,9},{9,8},{10,11... | collective-permute-start | bytes 1474568 | tf_op jit(solution)/shard_map/ppermute | solution.py:396
  10.5 35.7 %collective-permute-start.1 = (bf16[4,448,1024]{2,1,0:T(8,128)(2,1)}, bf16[4,448,1024]{2,1,0:T(8,128)(2,1)}, u32[]{:S(2)}, u32[]{:S(2)}) collective-permute-start(bf16[4,448,1024]{2,1,0:T(8,128)(2,1)} %shard_map.112), channel_id=1, source_target_pairs={{0,1},{1,0},{2,3},{3,2},{4,5},{5,4},{6,7},{7,6},{8,9},{9,8},{10,11... | collective-permute-start | bytes 11010056 | tf_op jit(solution)/shard_map/ppermute | solution.py:416
  32.1 14.1 %all-to-all-start.1 = ((bf16[32,48,128]{2,1,0:T(8,128)(2,1)}), bf16[32,48,128]{2,1,0:T(8,128)(2,1)S(1)}, u32[]{:S(2)}, u32[]{:S(2)}) async-start(bf16[32,48,128]{2,1,0:T(8,128)(2,1)} %get-tuple-element.37), calls=%async_computation.1 | async-start | bytes 786432 | tf_op jit(solution)/shard_map/all_to_all | solution.py:384
  38.2 7.9 %copy-start.2 = (s32[8]{0:T(128)}, s32[8]{0:T(128)S(1)}, u32[]{:S(2)}) copy-start(s32[8]{0:T(128)S(1)} %shard_map.113.oth) | copy-start | bytes 100
  46.1 0.7 copy-start.3
  70.2 4.3 %collective-permute-start.2 = (bf16[1,112,128]{2,1,0:T(8,128)(2,1)S(1)}, bf16[1,112,128]{2,1,0:T(8,128)(2,1)S(1)}, u32[]{:S(2)}, u32[]{:S(2)}) collective-permute-start(bf16[1,112,128]{2,1,0:T(8,128)(2,1)S(1)} %get-tuple-element.43), channel_id=1, source_target_pairs={{0,64},{64,0},{128,192},{192,128},{1,65},{65,1},{129,193},{193,129... | collective-permute-start | bytes 86024 | tf_op jit(solution)/shard_map/ppermute | solution.py:459
  74.5 6.2 %collective-permute-start.3 = (bf16[2,112,128]{2,1,0:T(8,128)(2,1)S(1)}, bf16[2,112,128]{2,1,0:T(8,128)(2,1)S(1)}, u32[]{:S(2)}, u32[]{:S(2)}) collective-permute-start(bf16[2,112,128]{2,1,0:T(8,128)(2,1)S(1)} %constant_dynamic-update-slice_fusion.first_ref), channel_id=1, source_target_pairs={{0,192},{64,128},{128,64},{192,0},{1,193},{65,129},{129,65},{193,1... | collective-permute-start | bytes 172040 | tf_op jit(solution)/shard_map/ppermute | solution.py:460
  82.1 11.6 %copy-start.1 = (bf16[4,32,1024]{2,1,0:T(8,128)(2,1)S(1)}, bf16[4,32,1024]{2,1,0:T(8,128)(2,1)}, u32[]{:S(2)}) copy-start(bf16[4,32,1024]{2,1,0:T(8,128)(2,1)} %get-tuple-element.45.own_ref) | copy-start | bytes 786436
  82.1 21.4 %all-to-all-start.3 = ((bf16[32,208,128]{2,1,0:T(8,128)(2,1)}), bf16[32,208,128]{2,1,0:T(8,128)(2,1)S(1)}, u32[]{:S(2)}, u32[]{:S(2)}) async-start(bf16[32,208,128]{2,1,0:T(8,128)(2,1)} %shard_map.118), calls=%async_computation.3 | async-start | bytes 3407872 | tf_op jit(solution)/shard_map/all_to_all | solution.py:384
  86.3 7.3 %collective-permute-start.4 = (bf16[4,32,1024]{2,1,0:T(8,128)(2,1)}, bf16[4,32,1024]{2,1,0:T(8,128)(2,1)S(1)}, u32[]{:S(2)}, u32[]{:S(2)}) collective-permute-start(bf16[4,32,1024]{2,1,0:T(8,128)(2,1)} %get-tuple-element.46), channel_id=1, source_target_pairs={{0,1},{1,0},{2,3},{3,2},{4,5},{5,4},{6,7},{7,6},{8,9},{9,8},{10,11... | collective-permute-start | bytes 786440 | tf_op jit(solution)/shard_map/ppermute | solution.py:440
  104.4 9.0 %collective-permute-start.5 = (bf16[80,3328]{1,0:T(8,128)(2,1)S(1)}, bf16[80,3328]{1,0:T(8,128)(2,1)S(1)}, u32[]{:S(2)}, u32[]{:S(2)}) collective-permute-start(bf16[80,3328]{1,0:T(8,128)(2,1)S(1)} %get-tuple-element.51), channel_id=1, source_target_pairs={{0,1},{1,0},{2,3},{3,2},{4,5},{5,4},{6,7},{7,6},{8,9},{9,8},{10,11... | collective-permute-start | bytes 1597448 | tf_op jit(solution)/shard_map/ppermute | solution.py:476

commit v3 on v2

--- a/solution.py
+++ b/solution.py
@@ -41,12 +41,9 @@
 
 
 def pack_w(core, length, owner, w_ref, q_ref, gain_ref, mine_ref, out_ref, info_ref):
-    lane = lax.broadcasted_iota(jnp.int32, (16, 128), 1)
-    values = jnp.zeros((16, 128), F32)
     for s in range(4):
-        for kind, value in enumerate((length[s // 2, s % 2], owner[s // 2, 0, s % 2])):
-            info_ref[4 * kind + s] = value
-            values = jnp.where(lane == 4 * kind + s, value.astype(F32), values)
+        info_ref[s] = length[s // 2, s % 2]
+        info_ref[4 + s] = owner[s // 2, 0, s % 2]
     info_ref[8] = core[0]
     for ref, half in ((out_ref, 1 - core[0]), (mine_ref, core[0])):
         for b in range(3):
@@ -54,7 +51,6 @@
         for j in range(4):
             ref[64:80, j * 128 : j * 128 + 64] = q_ref[j * 16 : (j + 1) * 16, :]
         ref[64:80, 512:576] = jnp.broadcast_to(gain_ref[...], (16, FEATS))
-        ref[64:80, 640:768] = values.astype(BF16)
 
 
 def pack_memory(core, keys_ref, values_ref, d_ref, out_ref):
@@ -66,13 +62,6 @@
 def unpack(ref):
     question = [ref[64:80, j * 128 : j * 128 + 64].astype(F32) for j in range(4)]
     return jnp.concatenate(question, axis=0), ref[64:80, 512:576].astype(F32)[0:1]
-
-
-def slots_of(recv_ref, info_ref):
-    values = recv_ref[64:80, 640:768].astype(F32)[0:1]
-    lane = lax.broadcasted_iota(jnp.int32, (1, 128), 1)
-    for i in range(8):
-        info_ref[i] = jnp.sum(jnp.where(lane == i, values, 0.0)).astype(jnp.int32)
 
 
 def project(mine_ref, recv_ref, part_ref, wc_ref, pair_ref, gains_ref):
@@ -93,24 +82,30 @@
                     rb * 16 : (rb + 1) * 16, t * 128 : (t + 1) * 128
                 ]
     squares = jnp.sum(pair * pair, axis=1, keepdims=True)
-    low = lax.broadcasted_iota(jnp.int32, (8, 128), 1) < 64
-    for rb in range(4):
-        tile = jnp.where(
-            low, squares[rb * 16 : rb * 16 + 8], squares[rb * 16 + 8 : rb * 16 + 16]
+    lane = lax.broadcasted_iota(jnp.int32, (8, 128), 1) // 16
+    tile = jnp.zeros((8, 128), F32)
+    for j in range(8):
+        tile = jnp.where(lane == j, squares[j * 8 : (j + 1) * 8], tile)
+    for k in range(CHIPS):
+        part_ref[k, CHUNK : CHUNK + 8, :] = tile
+
+
+def normalise(position, part_ref, qkv_ref, rate_ref, rates_ref):
+    total = jnp.sum(part_ref[...], axis=0)
+    tile = lax.rsqrt(total[CHUNK:] / D + EPS)
+    rates = [
+        jnp.broadcast_to(
+            jnp.concatenate([tile[:, j * 32 : j * 32 + 1], tile[:, j * 32 + 16 : j * 32 + 17]], axis=0),
+            (16, 128),
         )
-        for cb in range(COL_BLOCKS):
-            part_ref[rb * COL_BLOCKS + cb, CHUNK : CHUNK + 8, :] = tile
-
-
-def normalise(part_ref, qkv_ref, pre_ref, rate_ref):
-    total = jnp.sum(part_ref[...], axis=0)
-    rates = lax.rsqrt(total[CHUNK:] / D + EPS)
-    rate = jnp.concatenate([rates[:, 0:1], rates[:, 64:65]], axis=0)
-    rate = jnp.broadcast_to(rate, (16, 128))
-    pre = total[:CHUNK]
-    pre_ref[...] = pre
+        for j in range(4)
+    ]
+    rate = rates[0]
+    for j in range(4):
+        rates_ref[j * 16 : (j + 1) * 16] = rates[j]
+        rate = jnp.where(position[0] // (2 * COL_BLOCKS) == j, rates[j], rate)
     rate_ref[...] = rate
-    qkv = (pre * jnp.concatenate([rate] * 3, axis=0)).astype(BF16)
+    qkv = (total[:CHUNK] * jnp.concatenate([rate] * 3, axis=0)).astype(BF16)
     for k in range(CHIPS):
         qkv_ref[k] = qkv
 
@@ -138,7 +133,7 @@
             kcat[unit, 224:256] = jnp.zeros((32, 256), BF16)
             vcat[unit, 224:256] = jnp.zeros((32, 256), BF16)
 
-    key_at = lax.broadcasted_iota(jnp.int32, (1, 256), 1)
+    key_at = lax.broadcasted_iota(jnp.int32, (256, 1), 0)
     lane_head = lax.broadcasted_iota(jnp.int32, (QLEN, 256), 1) // 64
 
     def diagonal(full):
@@ -169,33 +164,31 @@
         d_rows[unit] = jnp.concatenate([d_out] * 4, axis=0) * mask_d[...]
     for side, hg in units:
         unit = side * 4 + hg
-        scores[unit] = dot(query[unit], kcat[unit], NT)
-        d_prob[unit] = dot(d_rows[unit], vcat[unit], NT)
+        scores[unit] = dot(kcat[unit], query[unit], NT)
+        d_prob[unit] = dot(vcat[unit], d_rows[unit], NT)
     for side, hg in units:
         unit = side * 4 + hg
         live = key_at < infos[side][step] + QLEN
-        for h in range(4):
-            part = slice(h * QLEN, (h + 1) * QLEN)
-            score = jnp.where(live, scores[unit, part], -1e30)
-            expo = jnp.exp(score - jnp.max(score, axis=1, keepdims=True))
-            prob = expo * (1.0 / jnp.sum(expo, axis=1, keepdims=True))
-            d_p = d_prob[unit, part]
-            inner = jnp.sum(d_p * prob, axis=1, keepdims=True)
-            prob_b[unit, part] = prob.astype(BF16)
-            d_scores[unit, part] = (prob * (d_p - inner)).astype(BF16)
+        score = jnp.where(live, scores[unit], -1e30)
+        expo = jnp.exp(score - jnp.max(score, axis=0, keepdims=True))
+        prob = expo * (1.0 / jnp.sum(expo, axis=0, keepdims=True))
+        d_p = d_prob[unit]
+        inner = jnp.sum(d_p * prob, axis=0, keepdims=True)
+        prob_b[unit] = prob.astype(BF16)
+        d_scores[unit] = (prob * (d_p - inner)).astype(BF16)
     for side, hg in units:
         unit = side * 4 + hg
         lanes = slice(hg * 256, (hg + 1) * 256)
         question = infos[side][4 + step]
-        context = diagonal(dot(prob_b[unit], vcat[unit])).astype(BF16)
+        context = diagonal(dot(prob_b[unit], vcat[unit], TN)).astype(BF16)
         if side == 0:
             ctx_own[0, :, lanes] = context
         else:
             ctx_oth[0, :, lanes] = context
         grads = (
-            diagonal(dot(d_scores[unit], kcat[unit])) * FOLD,
-            dot(d_scores[unit, :, 0:QLEN], query[unit], TN),
-            dot(prob_b[unit, :, 0:QLEN], d_rows[unit], TN),
+            diagonal(dot(d_scores[unit], kcat[unit], TN)) * FOLD,
+            dot(d_scores[unit, 0:QLEN], query[unit]),
+            dot(prob_b[unit, 0:QLEN], d_rows[unit]),
         )
         for kind, grad in enumerate(grads):
             for tt in range(2):
@@ -216,33 +209,22 @@
     out_ref[:, :, lanes_of(1 - core[0], HALF)] = theirs_ref[...]
 
 
-def split_rows(value):
-    high = value.astype(BF16).astype(F32)
-    low = lax.broadcasted_iota(jnp.int32, value.shape, 1) < 64
-    return jnp.where(low, high, value - high).astype(BF16)
-
-
-def finish_grad(recv_ref, pre_ref, rate_ref, pair_ref, out_ref, cubed_ref):
+def finish_grad(recv_ref, rate_ref, pair_ref, out_ref):
     grad = jnp.sum(recv_ref[...].astype(F32), axis=0)
-    rate = rate_ref[...]
-    product = grad * pre_ref[...]
-    product = product[0:16] + product[16:32] + product[32:48]
-    d_rate = jnp.sum(product, axis=1, keepdims=True)
-    cubed_ref[...] = split_rows(d_rate * rate * rate * rate)
-    out_ref[0, 0:CHUNK] = (grad * jnp.concatenate([rate] * 3, axis=0)).astype(BF16)
+    out_ref[0, 0:CHUNK] = (grad * jnp.concatenate([rate_ref[...]] * 3, axis=0)).astype(BF16)
     out_ref[0, CHUNK:] = pair_ref[...]
 
 
-def spread(first_ref, second_ref, cubed_ref, out_ref):
+def spread(first_ref, second_ref, out_ref):
     for k in range(CHIPS):
         for g in range(4):
             ref = first_ref if g < 2 else second_ref
             out_ref[k, g * CHUNK : (g + 1) * CHUNK] = ref[g % 2, 0:CHUNK]
-        out_ref[k, 4 * CHUNK :] = cubed_ref[...]
 
 
 def weight_grads(
-    recv_ref, first_ref, second_ref, gains_ref, wc_ref, send_ref, small_ref, d_pre, scaled, d_in
+    recv_ref, qkv_ref, first_ref, second_ref, gains_ref, wc_ref,
+    send_ref, small_ref, d_pre, scaled, d_in,
 ):
     pairs = [ref[g, CHUNK:] for ref in (first_ref, second_ref) for g in range(2)]
     pairs = jnp.concatenate(pairs, axis=0).astype(F32)
@@ -265,20 +247,23 @@
             d_in[...] = term
         else:
             d_in[...] += term
-    cubed = []
+    shares = []
     for rb in range(4):
         total = jnp.zeros((16, 128), F32)
         for cb in range(COL_BLOCKS):
-            total += recv_ref[rb * COL_BLOCKS + cb, 4 * CHUNK :].astype(F32)
-        cubed.append(total[:, 0:1] + total[:, 64:65])
-    cubed = jnp.broadcast_to(jnp.concatenate(cubed, axis=0), (ROWS, 128))
+            k = rb * COL_BLOCKS + cb
+            for t in range(3):
+                at = slice(t * 16, (t + 1) * 16)
+                total += recv_ref[k, at].astype(F32) * qkv_ref[k, at].astype(F32)
+        shares.append(jnp.sum(total, axis=1, keepdims=True))
+    share = jnp.broadcast_to(jnp.concatenate(shares, axis=0), (ROWS, 128))
     mine = d_in[0:ROWS]
     d_gain = jnp.broadcast_to(jnp.sum(pairs * d_in[...], axis=0, keepdims=True), (16, 128))
     low = lax.broadcasted_iota(jnp.int32, (ROWS, 128), 1) < 64
     small_ref[0:ROWS] = mine
-    small_ref[ROWS : 2 * ROWS] = cubed
+    small_ref[ROWS : 2 * ROWS] = share
     small_ref[2 * ROWS :] = d_gain
-    for value, at in ((jnp.where(low, cubed, mine), slice(0, 64)), (d_gain, slice(64, 80))):
+    for value, at in ((jnp.where(low, share, mine), slice(0, 64)), (d_gain, slice(64, 80))):
         high = value.astype(BF16)
         send_ref[at, COLS : COLS + 128] = high
         send_ref[at, COLS + 128 : COLS + 256] = (value - high.astype(F32)).astype(BF16)
@@ -305,7 +290,7 @@
         copy.wait()
 
 
-def finish(core, recv_ref, small_ref, mine_ref, in_ref, dq_ref, dg_ref, dw_ref, held, sems):
+def finish(core, recv_ref, small_ref, rates_ref, mine_ref, in_ref, dq_ref, dg_ref, dw_ref, held, sems):
     copies = columns_out(1 - core[0], held, dw_ref, sems)
     for b in range(3):
         at = slice(b * HALF, (b + 1) * HALF)
@@ -314,7 +299,7 @@
     theirs = recv_ref[:, COLS : COLS + 128].astype(F32)
     theirs += recv_ref[:, COLS + 128 : COLS + 256].astype(F32)
     d_input = small_ref[0:ROWS, 0:FEATS] + theirs[0:ROWS, 64:128]
-    cubed = small_ref[ROWS : 2 * ROWS, 0:1] + theirs[0:ROWS, 0:1]
+    cubed = rates_ref[:, 0:1] * (small_ref[ROWS : 2 * ROWS, 0:1] + theirs[0:ROWS, 0:1])
     question, gain = unpack(mine_ref)
     dq_ref[...] = (gain * d_input - cubed * question / D).astype(BF16)
     dg_ref[...] = small_ref[2 * ROWS : 2 * ROWS + 1, 0:FEATS] + theirs[ROWS : ROWS + 1, 64:128]
@@ -353,10 +338,10 @@
                 pltpu.VMEM((8, 256, 256), BF16),
                 pltpu.VMEM((8, 128, 256), BF16),
                 pltpu.VMEM((8, 128, 256), BF16),
-                pltpu.VMEM((8, 128, 256), F32),
-                pltpu.VMEM((8, 128, 256), F32),
-                pltpu.VMEM((8, 128, 256), BF16),
-                pltpu.VMEM((8, 128, 256), BF16),
+                pltpu.VMEM((8, 256, 128), F32),
+                pltpu.VMEM((8, 256, 128), F32),
+                pltpu.VMEM((8, 256, 128), BF16),
+                pltpu.VMEM((8, 256, 128), BF16),
                 pltpu.VMEM((CHIPS, CHUNK, 128), F32),
             ],
         ),
@@ -376,7 +361,8 @@
 
 
 def shards(question, norm_gain, w_qkv, mem_keys, mem_values, mem_length, owner, d_context):
-    core = jnp.reshape(lax.axis_index("passage") % 2, (1,)).astype(jnp.int32)
+    position = jnp.reshape(lax.axis_index("passage"), (1,)).astype(jnp.int32)
+    core = position % 2
     swap = [(i, i ^ 1) for i in range(2 * CHIPS)]
     same_core = [[c + 2 * i for i in range(CHIPS)] for c in range(2)]
 
@@ -393,7 +379,9 @@
         scalars=1,
         params=WIDE,
     )(core, mem_length, owner, w_qkv, q64, gain)
-    recv = lax.ppermute(sent, "passage", swap)
+    recv, other_info = lax.optimization_barrier(
+        (lax.ppermute(sent, "passage", swap), lax.ppermute(info, "passage", swap))
+    )
 
     memory_core, _ = lax.optimization_barrier((core, sent))
     half = lambda s, c: (s // 2, s % 2, 0, 1 - c[0])
@@ -425,13 +413,12 @@
         ],
         [VMEM] * 2,
     )(mine, recv)
-    (other_info,) = call(slots_of, [((8,), jnp.int32)], [VMEM], scalars=1)(recv)
     part = exchange(part)
-    qkv, pre, rate = call(
+    qkv, rate, rates = call(
         normalise,
-        [((CHIPS, CHUNK, 128), BF16), ((CHUNK, 128), F32), ((16, 128), F32)],
-        [VMEM],
-    )(part)
+        [((CHIPS, CHUNK, 128), BF16), ((16, 128), F32), ((ROWS, 128), F32)],
+        [SMEM, VMEM],
+    )(position, part)
     qkv = exchange(qkv)
 
     ctx_own, ctx_oth, grads = attention(
@@ -451,16 +438,10 @@
     )(core, ctx_own, ctx_mine)
 
     grads = exchange(grads)
-    chunk, cubed = call(
-        finish_grad,
-        [((1, CHUNK + ROWS, 128), BF16), ((16, 128), BF16)],
-        [VMEM] * 4,
-    )(grads, pre, rate, pair)
+    (chunk,) = call(finish_grad, [((1, CHUNK + ROWS, 128), BF16)], [VMEM] * 3)(grads, rate, pair)
     first = jnp.concatenate([chunk, lax.ppermute(chunk, "dp", [(g, g ^ 1) for g in range(4)])])
     second = lax.ppermute(first, "dp", [(g, g ^ 3) for g in range(4)])
-    (d_pre,) = call(spread, [((CHIPS, 4 * CHUNK + 16, 128), BF16)], [VMEM] * 3)(
-        first, second, cubed
-    )
+    (d_pre,) = call(spread, [((CHIPS, 4 * CHUNK, 128), BF16)], [VMEM] * 2)(first, second)
     d_pre, context = lax.optimization_barrier((exchange(d_pre), context))
     send, small, blocks, scaled = call(
         weight_grads,
@@ -470,9 +451,9 @@
             ((COL_BLOCKS, 4 * ROWS, 384), BF16),
             ((FEATS, 4 * ROWS), BF16),
         ],
-        [VMEM] * 5,
+        [VMEM] * 6,
         [pltpu.VMEM((4 * ROWS, 128), F32)],
-    )(d_pre, first, second, gains, wc)
+    )(d_pre, qkv, first, second, gains, wc)
     recv = lax.ppermute(send, "passage", swap)
     any_space = pl.BlockSpec(memory_space=pl.ANY)
     staging = [pltpu.VMEM((FEATS, COLS), F32), pltpu.SemaphoreType.DMA((3,))]
@@ -491,12 +472,12 @@
             jax.ShapeDtypeStruct((1, FEATS), F32),
             jax.ShapeDtypeStruct((FEATS, 2 * COLS), F32),
         ],
-        in_specs=[SMEM] + [VMEM] * 3 + [any_space],
+        in_specs=[SMEM] + [VMEM] * 4 + [any_space],
         out_specs=[VMEM, VMEM, any_space],
         scratch_shapes=staging,
-        input_output_aliases={4: 2},
+        input_output_aliases={5: 2},
         compiler_params=PARAMS,
-    )(core, recv, small, mine, d_weight)
+    )(core, recv, small, rates, mine, d_weight)
     return (
         context.reshape(2, 2, QLEN, 2 * HALF),
         d_question.reshape(question.shape),

time: 115 us -> 113 us (0.983)
  blocking collectives: 32.9 us -> 47.5 us
  waiting for transfers between devices: 21.5 us -> 12 us
  starting transfers between devices: 33.9 us -> 28.4 us
  Pallas kernels: 25.1 us -> 23.1 us
    all_to_all x2 -> x3, blocking collectives: 32.9 us -> 47.5 us  [exchange(): lax.all_to_all(x, 'passage', 0, 0, tiled=True, axis_index_groups=same_core)]
    all_to_all x2 -> x1, waiting for transfers between devices: 16.9 us -> 7.37 us  [exchange(): lax.all_to_all(x, 'passage', 0, 0, tiled=True, axis_index_groups=same_core)]
    all_to_all x2 -> x1, starting transfers between devices: 9.64 us -> 4.3 us  [exchange(): lax.all_to_all(x, 'passage', 0, 0, tiled=True, axis_index_groups=same_core)]
    pallas_call x4 -> x3, Pallas kernels: 3.26 us -> 1.62 us  [the longest x1 1.35 us: shards(): call(spread, [((CHIPS, 4 * CHUNK, 128), BF16)], [VMEM] * 2)(first, second)]
    ppermute x1 -> x2, starting transfers between devices: 3.33 us -> 3.44 us  [the longest x1 3.33 us: shards(): lax.ppermute(sent, 'passage', swap)]
  transfers between devices with their start and end apart: 8 -> 8, of which waited for: 6 -> 5; matrix products, arithmetic and copies ran while one was open for 0% -> 0% of each run, Pallas kernels for 7% -> 6%
where the time goes in v3:
time: 113 us
  blocking collectives  47.5 us (42%)
  starting transfers between devices  28.4 us (25%)
  Pallas kernels  23.1 us (20%)
  waiting for transfers between devices  12 us (11%)
    all_to_all x3, blocking collectives, exchange(): lax.all_to_all(x, 'passage', 0, 0, tiled=True, axis_index_groups=same_core)  47.5 us
    pallas_call x1, Pallas kernels, attention(): pl.pallas_call(attend, out_shape=[jax.ShapeDtypeStruct((4, QLEN, HALF), B...  9.93 us
    all_to_all x1, waiting for transfers between devices, exchange(): lax.all_to_all(x, 'passage', 0, 0, tiled=True, axis_index_groups=same_core)  7.37 us
    ppermute x1, starting transfers between devices, shards(): recv = lax.ppermute(send, 'passage', swap)  6.95 us
    ppermute x1, starting transfers between devices, shards(): ctx_mine = lax.ppermute(ctx_oth, 'passage', swap)  5.6 us
    ppermute x1, starting transfers between devices, shards(): second = lax.ppermute(first, 'dp', [(g, g ^ 3) for g in range(4)])  4.57 us
    pallas_call x1, Pallas kernels, shards(): pl.pallas_call(pack_memory, out_shape=jax.ShapeDtypeStruct((4, PACKED, HA...  4.36 us
    all_to_all x1, starting transfers between devices, exchange(): lax.all_to_all(x, 'passage', 0, 0, tiled=True, axis_index_groups=same_core)  4.3 us
  transfers between devices with their start and end apart: 8, of which 5 were waited for; matrix products, arithmetic and copies ran while one was open for 0% of the time, Pallas kernels for 6%

profile of v3, /device:TPU:1, one launch (start us, length us, event | category | flops | bytes accessed | tf_op | source)
XLA Modules:
  0.0 112.6 jit_solution(457590815536338650)
XLA Ops:
  0.6 2.2 %shard_map.111 = (bf16[80,3072]{1,0:T(8,128)(2,1)}, bf16[80,3072]{1,0:T(8,128)(2,1)}, s32[9]{0:T(128)}) custom-call(s32[1]{0:T(128)S(6)} %select_n.7.core, s32[2,2]{1,0:T(2,128)} %length.1, s32[2,1,2]{2,1,0:T(1,128)} %owner.1, bf16[64,6144]{1,0:T(8,128)(2,1)} %w_ref.1, bf16[64,64]{1,0:T(8,128)(2,1)} %bitcast.7, bf16[1,64]{1,0:T(2,128)(2,1)} %bitcast.8), custom_call_target="tpu_custom_call" | custom-call | tf_op jit(solution)/shard_map/pallas_call | solution.py:375
  2.8 3.3 %collective-permute-start = (bf16[80,3072]{1,0:T(8,128)(2,1)}, bf16[80,3072]{1,0:T(8,128)(2,1)S(1)}, u32[]{:S(2)}, u32[]{:S(2)}) collective-permute-start(bf16[80,3072]{1,0:T(8,128)(2,1)} %get-tuple-element.32), channel_id=1, source_target_pairs={{0,1},{1,0},{2,3},{3,2},{4,5},{5,4},{6,7},{7,6},{8,9},{9,8},{10,11... | collective-permute-start | bytes 1474568 | tf_op jit(solution)/shard_map/ppermute | solution.py:383
  6.3 4.4 %shard_map.112 = bf16[4,448,1024]{2,1,0:T(8,128)(2,1)} custom-call(s32[1]{0:T(128)S(6)} %select_n.7.core, bf16[2,2,200,2048]{3,2,1,0:T(8,128)(2,1)} %keys_ref.3, bf16[2,2,200,2048]{3,2,1,0:T(8,128)(2,1)} %values_ref.3, bf16[2,2,32,2048]{3,2,1,0:T(8,128)(2,1)} %d_ref.3), custom_call_target="tpu_custom_call" | custom-call | tf_op jit(solution)/shard_map/pallas_call | solution.py:388
  10.6 0.5 collective-permute-start.2
  11.1 0.3 shard_map.113
  11.4 20.4 %all_to_all.20.part_ref = f32[32,56,128]{2,1,0:T(8,128)S(1)} all-to-all(f32[32,56,128]{2,1,0:T(8,128)S(1)} %get-tuple-element.38), channel_id=1, replica_groups={{0,2,4,6,8,10,12,14,16,18,20,22,24,26,28,30,32,34,36,38,40,42,44,46,48,..., dimensions={0} | all-to-all | bytes 1835008 | tf_op jit(solution)/shard_map/all_to_all | solution.py:370
  32.1 14.1 %all_to_all.21.qkv_ref = bf16[32,48,128]{2,1,0:T(8,128)(2,1)} all-to-all(bf16[32,48,128]{2,1,0:T(8,128)(2,1)S(1)} %get-tuple-element.39), channel_id=1, replica_groups={{0,2,4,6,8,10,12,14,16,18,20,22,24,26,28,30,32,34,36,38,40,42,44,46,48,..., dimensions={0} | all-to-all | bytes 786432 | tf_op jit(solution)/shard_map/all_to_all | solution.py:370
  46.2 9.9 %shard_map.115 = (bf16[4,32,1024]{2,1,0:T(8,128)(2,1)}, bf16[4,32,1024]{2,1,0:T(8,128)(2,1)}, bf16[32,48,128]{2,1,0:T(8,128)(2,1)}) custom-call(s32[9]{0:T(128)} %get-tuple-element.31.own, s32[9]{0:T(128)} %copy-done.3, bf16[32,48,128]{2,1,0:T(8,128)(2,1)} %all_to_all.21.qkv_ref, bf16[2,2,200,2048]{3,2,1,0:T(8,128)(2,1)} %keys_ref.3, ...), custom_call_target="tpu_custom_call" | custom-call | tf_op jit(solution)/shard_map/pallas_call | solution.py:311
  56.2 12.9 %all_to_all.22.recv_ref = bf16[32,48,128]{2,1,0:T(8,128)(2,1)S(1)} all-to-all(bf16[32,48,128]{2,1,0:T(8,128)(2,1)} %get-tuple-element.41), channel_id=1, replica_groups={{0,2,4,6,8,10,12,14,16,18,20,22,24,26,28,30,32,34,36,38,40,42,44,46,48,..., dimensions={0} | all-to-all | bytes 786432 | tf_op jit(solution)/shard_map/all_to_all | solution.py:370
  69.1 3.1 %collective-permute-start.3 = (bf16[1,112,128]{2,1,0:T(8,128)(2,1)S(1)}, bf16[1,112,128]{2,1,0:T(8,128)(2,1)S(1)}, u32[]{:S(2)}, u32[]{:S(2)}) collective-permute-start(bf16[1,112,128]{2,1,0:T(8,128)(2,1)S(1)} %shard_map.116), channel_id=1, source_target_pairs={{0,64},{64,0},{128,192},{192,128},{1,65},{65,1},{129,193},{193,129... | collective-permute-start | bytes 86024 | tf_op jit(solution)/shard_map/ppermute | solution.py:442
  72.2 1.3 %collective-permute-done.3 = bf16[1,112,128]{2,1,0:T(8,128)(2,1)S(1)} collective-permute-done((bf16[1,112,128]{2,1,0:T(8,128)(2,1)S(1)}, bf16[1,112,128]{2,1,0:T(8,128)(2,1)S(1)}, u32[]{:S(2)}, u32[]{:S(2)}) %collective-permute-start.3) | collective-permute-done | bytes 28704 | tf_op jit(solution)/shard_map/ppermute | solution.py:442
  73.5 4.6 %collective-permute-start.4 = (bf16[2,112,128]{2,1,0:T(8,128)(2,1)S(1)}, bf16[2,112,128]{2,1,0:T(8,128)(2,1)S(1)}, u32[]{:S(2)}, u32[]{:S(2)}) collective-permute-start(bf16[2,112,128]{2,1,0:T(8,128)(2,1)S(1)} %pad_maximum_fusion.first_ref), channel_id=1, source_target_pairs={{0,192},{64,128},{128,64},{192,0},{1,193},{65,129},{129,65},{193,1... | collective-permute-start | bytes 172040 | tf_op jit(solution)/shard_map/ppermute | solution.py:443
  78.0 1.7 %collective-permute-done.4.second_ref = bf16[2,112,128]{2,1,0:T(8,128)(2,1)S(1)} collective-permute-done((bf16[2,112,128]{2,1,0:T(8,128)(2,1)S(1)}, bf16[2,112,128]{2,1,0:T(8,128)(2,1)S(1)}, u32[]{:S(2)}, u32[]{:S(2)}) %collective-permute-start.4) | collective-permute-done | bytes 57376 | tf_op jit(solution)/shard_map/ppermute | solution.py:443
  79.7 1.3 %shard_map.117 = bf16[32,192,128]{2,1,0:T(8,128)(2,1)} custom-call(bf16[2,112,128]{2,1,0:T(8,128)(2,1)S(1)} %pad_maximum_fusion.first_ref, bf16[2,112,128]{2,1,0:T(8,128)(2,1)S(1)} %collective-permute-done.4.second_ref), custom_call_target="tpu_custom_call" | custom-call | tf_op jit(solution)/shard_map/pallas_call | solution.py:444
  81.1 4.3 %all-to-all-start.3 = ((bf16[32,192,128]{2,1,0:T(8,128)(2,1)}), bf16[32,192,128]{2,1,0:T(8,128)(2,1)S(1)}, u32[]{:S(2)}, u32[]{:S(2)}) async-start(bf16[32,192,128]{2,1,0:T(8,128)(2,1)} %shard_map.117), calls=%async_computation.3 | async-start | bytes 3145728 | tf_op jit(solution)/shard_map/all_to_all | solution.py:370
  85.4 5.6 %collective-permute-start.5 = (bf16[4,32,1024]{2,1,0:T(8,128)(2,1)}, bf16[4,32,1024]{2,1,0:T(8,128)(2,1)S(1)}, u32[]{:S(2)}, u32[]{:S(2)}) collective-permute-start(bf16[4,32,1024]{2,1,0:T(8,128)(2,1)} %get-tuple-element.45), channel_id=1, source_target_pairs={{0,1},{1,0},{2,3},{3,2},{4,5},{5,4},{6,7},{7,6},{8,9},{9,8},{10,11... | collective-permute-start | bytes 786440 | tf_op jit(solution)/shard_map/ppermute | solution.py:427
  91.0 1.4 %collective-permute-done.5.theirs_ref = bf16[4,32,1024]{2,1,0:T(8,128)(2,1)S(1)} collective-permute-done((bf16[4,32,1024]{2,1,0:T(8,128)(2,1)}, bf16[4,32,1024]{2,1,0:T(8,128)(2,1)S(1)}, u32[]{:S(2)}, u32[]{:S(2)}) %collective-permute-start.5) | collective-permute-done | bytes 262176 | tf_op jit(solution)/shard_map/ppermute | solution.py:427
  92.3 0.9 copy-done.2
  93.3 0.8 shard_map.118
  94.1 7.4 %all-to-all-done.3.recv_ref = bf16[32,192,128]{2,1,0:T(8,128)(2,1)S(1)} async-done(((bf16[32,192,128]{2,1,0:T(8,128)(2,1)}), bf16[32,192,128]{2,1,0:T(8,128)(2,1)S(1)}, u32[]{:S(2)}, u32[]{:S(2)}) %all-to-all-start.3) | async-done | bytes 1572896 | tf_op jit(solution)/shard_map/all_to_all | solution.py:370
  101.5 1.0 shard_map.119
  102.5 7.0 %collective-permute-start.6 = (bf16[80,3328]{1,0:T(8,128)(2,1)S(1)}, bf16[80,3328]{1,0:T(8,128)(2,1)S(1)}, u32[]{:S(2)}, u32[]{:S(2)}) collective-permute-start(bf16[80,3328]{1,0:T(8,128)(2,1)S(1)} %get-tuple-element.50), channel_id=1, source_target_pairs={{0,1},{1,0},{2,3},{3,2},{4,5},{5,4},{6,7},{7,6},{8,9},{9,8},{10,11... | collective-permute-start | bytes 1597448 | tf_op jit(solution)/shard_map/ppermute | solution.py:457
  109.5 1.2 %shard_map.120.in_ref = f32[64,6144]{1,0:T(8,128)} custom-call(s32[1]{0:T(128)S(6)} %select_n.7.core, bf16[8,256,384]{2,1,0:T(8,128)(2,1)S(1)} %get-tuple-element.53.d_pre_ref, bf16[64,256]{1,0:T(8,128)(2,1)S(1)} %get-tuple-element.54.scaled_ref), custom_call_target="tpu_custom_call" | custom-call | tf_op jit(solution)/shard_map/pallas_call | solution.py:460
  111.0 1.5 %shard_map.121 = (bf16[64,64]{1,0:T(8,128)(2,1)}, f32[1,64]{1,0:T(1,128)}, f32[64,6144]{1,0:T(8,128)}) custom-call(s32[1]{0:T(128)S(6)} %select_n.7.core, bf16[80,3328]{1,0:T(8,128)(2,1)S(1)} %collective-permute-done.6.recv_ref, f32[144,128]{1,0:T(8,128)S(1)} %get-tuple-element.51.small_ref, ...), custom_call_target="tpu_custom_call", output_to_operand_aliasing={{2}: (5, {})} | custom-call | tf_op jit(solution)/shard_map/pallas_call | solution.py:468
  (15 shorter events, 0.7 us)
Async XLA Ops:
  2.8 7.8 %collective-permute-start = (bf16[80,3072]{1,0:T(8,128)(2,1)}, bf16[80,3072]{1,0:T(8,128)(2,1)S(1)}, u32[]{:S(2)}, u32[]{:S(2)}) collective-permute-start(bf16[80,3072]{1,0:T(8,128)(2,1)} %get-tuple-element.32), channel_id=1, source_target_pairs={{0,1},{1,0},{2,3},{3,2},{4,5},{5,4},{6,7},{7,6},{8,9},{9,8},{10,11... | collective-permute-start | bytes 1474568 | tf_op jit(solution)/shard_map/ppermute | solution.py:383
  6.1 4.9 %copy-start.1 = (bf16[80,3072]{1,0:T(8,128)(2,1)S(1)}, bf16[80,3072]{1,0:T(8,128)(2,1)}, u32[]{:S(2)}) copy-start(bf16[80,3072]{1,0:T(8,128)(2,1)} %get-tuple-element.34.mine_ref) | copy-start | bytes 1474564
  6.2 4.5 %collective-permute-start.1 = (s32[9]{0:T(128)}, s32[9]{0:T(128)S(1)}, u32[]{:S(2)}, u32[]{:S(2)}) collective-permute-start(s32[9]{0:T(128)} %get-tuple-element.31.own), channel_id=1, source_target_pairs={{0,1},{1,0},{2,3},{3,2},{4,5},{5,4},{6,7},{7,6},{8,9},{9,8},{10,11... | collective-permute-start | bytes 116 | tf_op jit(solution)/shard_map/ppermute | solution.py:383
  10.6 21.5 %copy-start.3 = (s32[9]{0:T(128)}, s32[9]{0:T(128)S(1)}, u32[]{:S(2)}) copy-start(s32[9]{0:T(128)S(1)} %collective-permute-done.1.oth) | copy-start | bytes 112
  10.6 35.6 %collective-permute-start.2 = (bf16[4,448,1024]{2,1,0:T(8,128)(2,1)}, bf16[4,448,1024]{2,1,0:T(8,128)(2,1)}, u32[]{:S(2)}, u32[]{:S(2)}) collective-permute-start(bf16[4,448,1024]{2,1,0:T(8,128)(2,1)} %shard_map.112), channel_id=1, source_target_pairs={{0,1},{1,0},{2,3},{3,2},{4,5},{5,4},{6,7},{7,6},{8,9},{9,8},{10,11... | collective-permute-start | bytes 11010056 | tf_op jit(solution)/shard_map/ppermute | solution.py:404
  69.1 4.3 %collective-permute-start.3 = (bf16[1,112,128]{2,1,0:T(8,128)(2,1)S(1)}, bf16[1,112,128]{2,1,0:T(8,128)(2,1)S(1)}, u32[]{:S(2)}, u32[]{:S(2)}) collective-permute-start(bf16[1,112,128]{2,1,0:T(8,128)(2,1)S(1)} %shard_map.116), channel_id=1, source_target_pairs={{0,64},{64,0},{128,192},{192,128},{1,65},{65,1},{129,193},{193,129... | collective-permute-start | bytes 86024 | tf_op jit(solution)/shard_map/ppermute | solution.py:442
  73.5 6.2 %collective-permute-start.4 = (bf16[2,112,128]{2,1,0:T(8,128)(2,1)S(1)}, bf16[2,112,128]{2,1,0:T(8,128)(2,1)S(1)}, u32[]{:S(2)}, u32[]{:S(2)}) collective-permute-start(bf16[2,112,128]{2,1,0:T(8,128)(2,1)S(1)} %pad_maximum_fusion.first_ref), channel_id=1, source_target_pairs={{0,192},{64,128},{128,64},{192,0},{1,193},{65,129},{129,65},{193,1... | collective-permute-start | bytes 172040 | tf_op jit(solution)/shard_map/ppermute | solution.py:443
  81.1 20.4 %copy-start = (bf16[32,48,128]{2,1,0:T(8,128)(2,1)S(1)}, bf16[32,48,128]{2,1,0:T(8,128)(2,1)}, u32[]{:S(2)}) copy-start(bf16[32,48,128]{2,1,0:T(8,128)(2,1)} %all_to_all.21.qkv_ref) | copy-start | bytes 1179652
  81.1 20.4 %all-to-all-start.3 = ((bf16[32,192,128]{2,1,0:T(8,128)(2,1)}), bf16[32,192,128]{2,1,0:T(8,128)(2,1)S(1)}, u32[]{:S(2)}, u32[]{:S(2)}) async-start(bf16[32,192,128]{2,1,0:T(8,128)(2,1)} %shard_map.117), calls=%async_computation.3 | async-start | bytes 3145728 | tf_op jit(solution)/shard_map/all_to_all | solution.py:370
  85.4 7.0 %collective-permute-start.5 = (bf16[4,32,1024]{2,1,0:T(8,128)(2,1)}, bf16[4,32,1024]{2,1,0:T(8,128)(2,1)S(1)}, u32[]{:S(2)}, u32[]{:S(2)}) collective-permute-start(bf16[4,32,1024]{2,1,0:T(8,128)(2,1)} %get-tuple-element.45), channel_id=1, source_target_pairs={{0,1},{1,0},{2,3},{3,2},{4,5},{5,4},{6,7},{7,6},{8,9},{9,8},{10,11... | collective-permute-start | bytes 786440 | tf_op jit(solution)/shard_map/ppermute | solution.py:427
  92.3 0.9 copy-start.2
  102.5 8.5 %collective-permute-start.6 = (bf16[80,3328]{1,0:T(8,128)(2,1)S(1)}, bf16[80,3328]{1,0:T(8,128)(2,1)S(1)}, u32[]{:S(2)}, u32[]{:S(2)}) collective-permute-start(bf16[80,3328]{1,0:T(8,128)(2,1)S(1)} %get-tuple-element.50), channel_id=1, source_target_pairs={{0,1},{1,0},{2,3},{3,2},{4,5},{5,4},{6,7},{7,6},{8,9},{9,8},{10,11... | collective-permute-start | bytes 1597448 | tf_op jit(solution)/shard_map/ppermute | solution.py:457

commit v4 on v3

--- a/solution.py
+++ b/solution.py
@@ -18,7 +18,6 @@
 CHIPS = 32
 COL_BLOCKS = 8
 CHUNK = 48
-K_AT, V_AT, PACKED = 32, 240, 448
 FOLD = 0.125
 
 BF16 = jnp.bfloat16
@@ -38,6 +37,23 @@
 
 def lanes_of(index, width):
     return pl.ds(pl.multiple_of(index * width, width), width)
+
+
+def relay(source, stage, target, sems):
+    return (
+        pltpu.make_async_copy(source, stage, sems.at[0]),
+        pltpu.make_async_copy(stage, target, sems.at[1]),
+    )
+
+
+def run_relays(relays):
+    for first, _ in relays:
+        first.start()
+    for first, second in relays:
+        first.wait()
+        second.start()
+    for _, second in relays:
+        second.wait()
 
 
 def pack_w(core, length, owner, w_ref, q_ref, gain_ref, mine_ref, out_ref, info_ref):
@@ -53,10 +69,17 @@
         ref[64:80, 512:576] = jnp.broadcast_to(gain_ref[...], (16, FEATS))
 
 
-def pack_memory(core, keys_ref, values_ref, d_ref, out_ref):
-    out_ref[0, 0:QLEN] = d_ref[0, 0]
-    out_ref[0, K_AT : K_AT + MEM] = keys_ref[0, 0]
-    out_ref[0, V_AT : V_AT + MEM] = values_ref[0, 0]
+def pack_memory(core, keys_hbm, values_hbm, d_hbm, out_hbm, stage, d_stage, sems):
+    lanes = lanes_of(1 - core[0], HALF)
+    relays = []
+    for s in range(4):
+        slot = (s // 2, s % 2, slice(None), lanes)
+        relays += [
+            relay(keys_hbm.at[slot], stage.at[s, 0], out_hbm.at[s, 0], sems.at[s, 0]),
+            relay(values_hbm.at[slot], stage.at[s, 1], out_hbm.at[s, 1], sems.at[s, 1]),
+            relay(d_hbm.at[slot], d_stage.at[s], out_hbm.at[s, 2, 0:QLEN], sems.at[s, 2]),
+        ]
+    run_relays(relays)
 
 
 def unpack(ref):
@@ -111,7 +134,7 @@
 
 
 def attend(
-    own, oth, qkv_ref, keys_ref, values_ref, d_ref, packed_ref, ctx_own, ctx_oth, grad_ref,
+    own, oth, qkv_ref, keys_ref, values_ref, d_ref, packed_ref, packed_d_ref, ctx_own, ctx_oth, grad_ref,
     rows, mask_q, mask_d, kcat, vcat, query, d_rows, scores, d_prob, prob_b, d_scores, total,
 ):
     step = pl.program_id(0)
@@ -157,9 +180,9 @@
             vc[QLEN : QLEN + MEM] = values_ref[0, 0, :, lanes]
             d_out = d_ref[0, 0, :, lanes]
         else:
-            kc[QLEN : QLEN + MEM] = packed_ref[0, K_AT : K_AT + MEM, lanes]
-            vc[QLEN : QLEN + MEM] = packed_ref[0, V_AT : V_AT + MEM, lanes]
-            d_out = packed_ref[0, 0:QLEN, lanes]
+            kc[QLEN : QLEN + MEM] = packed_ref[0, 0, :, lanes]
+            vc[QLEN : QLEN + MEM] = packed_ref[0, 1, :, lanes]
+            d_out = packed_d_ref[0, 0, :, lanes]
         query[unit] = jnp.concatenate([rows[at, lanes]] * 4, axis=0) * mask_q[...]
         d_rows[unit] = jnp.concatenate([d_out] * 4, axis=0) * mask_d[...]
     for side, hg in units:
@@ -323,7 +346,8 @@
                 pl.BlockSpec((1, 1, MEM, HALF), lambda s, c, o: (s // 2, s % 2, 0, c[8])),
                 pl.BlockSpec((1, 1, MEM, HALF), lambda s, c, o: (s // 2, s % 2, 0, c[8])),
                 pl.BlockSpec((1, 1, QLEN, HALF), lambda s, c, o: (s // 2, s % 2, 0, c[8])),
-                pl.BlockSpec((1, PACKED, HALF), lambda s, c, o: (s, 0, 0)),
+                pl.BlockSpec((1, 2, MEM, HALF), lambda s, c, o: (s, 0, 0, 0)),
+                pl.BlockSpec((1, 1, QLEN, HALF), lambda s, c, o: (s, 2, 0, 0)),
             ],
             out_specs=[
                 pl.BlockSpec((1, QLEN, HALF), lambda s, c, o: (s, 0, 0)),
@@ -346,7 +370,7 @@
             ],
         ),
         compiler_params=WIDE,
-    )(own_info, other_info, qkv, mem_keys, mem_values, d_context, packed)
+    )(own_info, other_info, qkv, mem_keys, mem_values, d_context, packed, packed)
 
 
 def call(body, outs, specs, scratch=(), scalars=0, params=PARAMS):
@@ -372,6 +396,7 @@
     q64 = question.reshape(ROWS, FEATS)
     gain = norm_gain.reshape(1, FEATS)
 
+    any_space = pl.BlockSpec(memory_space=pl.ANY)
     mine, sent, info = call(
         pack_w,
         [((80, COLS), BF16), ((80, COLS), BF16), ((9,), jnp.int32)],
@@ -384,20 +409,16 @@
     )
 
     memory_core, _ = lax.optimization_barrier((core, sent))
-    half = lambda s, c: (s // 2, s % 2, 0, 1 - c[0])
     packed = pl.pallas_call(
         pack_memory,
-        out_shape=jax.ShapeDtypeStruct((4, PACKED, HALF), BF16),
-        grid_spec=pltpu.PrefetchScalarGridSpec(
-            num_scalar_prefetch=1,
-            grid=(4,),
-            in_specs=[
-                pl.BlockSpec((1, 1, MEM, HALF), half),
-                pl.BlockSpec((1, 1, MEM, HALF), half),
-                pl.BlockSpec((1, 1, QLEN, HALF), half),
-            ],
-            out_specs=pl.BlockSpec((1, PACKED, HALF), lambda s, c: (s, 0, 0)),
-        ),
+        out_shape=jax.ShapeDtypeStruct((4, 3, MEM, HALF), BF16),
+        in_specs=[SMEM] + [any_space] * 3,
+        out_specs=any_space,
+        scratch_shapes=[
+            pltpu.VMEM((4, 2, MEM, HALF), BF16),
+            pltpu.VMEM((4, QLEN, HALF), BF16),
+            pltpu.SemaphoreType.DMA((4, 3, 2)),
+        ],
         compiler_params=WIDE,
     )(memory_core, mem_keys, mem_values, d_context)
     packed, recv = lax.optimization_barrier((packed, recv))
@@ -455,7 +476,6 @@
         [pltpu.VMEM((4 * ROWS, 128), F32)],
     )(d_pre, qkv, first, second, gains, wc)
     recv = lax.ppermute(send, "passage", swap)
-    any_space = pl.BlockSpec(memory_space=pl.ANY)
     staging = [pltpu.VMEM((FEATS, COLS), F32), pltpu.SemaphoreType.DMA((3,))]
     d_weight = pl.pallas_call(
         own_weight,

time: 113 us -> 112 us (level)
    pallas_call x1, Pallas kernels: 4.36 us -> 3.1 us  [shards(): pl.pallas_call(pack_memory, out_shape=jax.ShapeDtypeStruct((4, 3, MEM, HA...]
  transfers between devices with their start and end apart: 8 -> 8, of which waited for: 5 -> 5; matrix products, arithmetic and copies ran while one was open for 0% -> 0% of each run, Pallas kernels for 6% -> 5%
where the time goes in v4:
time: 112 us
  blocking collectives  47.5 us (42%)
  starting transfers between devices  28.4 us (25%)
  Pallas kernels  22.1 us (20%)
  waiting for transfers between devices  12 us (11%)
    all_to_all x3, blocking collectives, exchange(): lax.all_to_all(x, 'passage', 0, 0, tiled=True, axis_index_groups=same_core)  47.5 us
    pallas_call x1, Pallas kernels, attention(): pl.pallas_call(attend, out_shape=[jax.ShapeDtypeStruct((4, QLEN, HALF), B...  10.2 us
    all_to_all x1, waiting for transfers between devices, exchange(): lax.all_to_all(x, 'passage', 0, 0, tiled=True, axis_index_groups=same_core)  7.37 us
    ppermute x1, starting transfers between devices, shards(): recv = lax.ppermute(send, 'passage', swap)  6.96 us
    ppermute x1, starting transfers between devices, shards(): ctx_mine = lax.ppermute(ctx_oth, 'passage', swap)  5.6 us
    ppermute x1, starting transfers between devices, shards(): second = lax.ppermute(first, 'dp', [(g, g ^ 3) for g in range(4)])  4.57 us
    all_to_all x1, starting transfers between devices, exchange(): lax.all_to_all(x, 'passage', 0, 0, tiled=True, axis_index_groups=same_core)  4.3 us
    ppermute x1, starting transfers between devices, shards(): lax.ppermute(sent, 'passage', swap)  3.33 us
  transfers between devices with their start and end apart: 8, of which 5 were waited for; matrix products, arithmetic and copies ran while one was open for 0% of the time, Pallas kernels for 5%

profile of v4, /device:TPU:1, one launch (start us, length us, event | category | flops | bytes accessed | tf_op | source)
XLA Modules:
  0.0 111.6 jit_solution(5085679573299989909)
XLA Ops:
  0.6 2.2 %shard_map.111 = (bf16[80,3072]{1,0:T(8,128)(2,1)}, bf16[80,3072]{1,0:T(8,128)(2,1)}, s32[9]{0:T(128)}) custom-call(s32[1]{0:T(128)S(6)} %select_n.7.core, s32[2,2]{1,0:T(2,128)} %length.1, s32[2,1,2]{2,1,0:T(1,128)} %owner.1, bf16[64,6144]{1,0:T(8,128)(2,1)} %w_ref.1, bf16[64,64]{1,0:T(8,128)(2,1)} %bitcast.7, bf16[1,64]{1,0:T(2,128)(2,1)} %bitcast.8), custom_call_target="tpu_custom_call" | custom-call | tf_op jit(solution)/shard_map/pallas_call | solution.py:400
  2.8 3.3 %collective-permute-start = (bf16[80,3072]{1,0:T(8,128)(2,1)}, bf16[80,3072]{1,0:T(8,128)(2,1)S(1)}, u32[]{:S(2)}, u32[]{:S(2)}) collective-permute-start(bf16[80,3072]{1,0:T(8,128)(2,1)} %get-tuple-element.32), channel_id=1, source_target_pairs={{0,1},{1,0},{2,3},{3,2},{4,5},{5,4},{6,7},{7,6},{8,9},{9,8},{10,11... | collective-permute-start | bytes 1474568 | tf_op jit(solution)/shard_map/ppermute | solution.py:408
  6.3 3.1 %shard_map.112 = bf16[4,3,200,1024]{3,2,1,0:T(8,128)(2,1)} custom-call(s32[1]{0:T(128)S(6)} %select_n.7.core, bf16[2,2,200,2048]{3,2,1,0:T(8,128)(2,1)} %keys_ref.1, bf16[2,2,200,2048]{3,2,1,0:T(8,128)(2,1)} %values_ref.1, bf16[2,2,32,2048]{3,2,1,0:T(8,128)(2,1)} %d_ref.1), custom_call_target="tpu_custom_call" | custom-call | tf_op jit(solution)/shard_map/pallas_call | solution.py:412
  9.4 0.5 collective-permute-start.2
  9.9 0.3 shard_map.113
  10.2 20.4 %all_to_all.20.part_ref = f32[32,56,128]{2,1,0:T(8,128)S(1)} all-to-all(f32[32,56,128]{2,1,0:T(8,128)S(1)} %get-tuple-element.38), channel_id=1, replica_groups={{0,2,4,6,8,10,12,14,16,18,20,22,24,26,28,30,32,34,36,38,40,42,44,46,48,..., dimensions={0} | all-to-all | bytes 1835008 | tf_op jit(solution)/shard_map/all_to_all | solution.py:394
  30.9 14.1 %all_to_all.21.qkv_ref = bf16[32,48,128]{2,1,0:T(8,128)(2,1)} all-to-all(bf16[32,48,128]{2,1,0:T(8,128)(2,1)S(1)} %get-tuple-element.39), channel_id=1, replica_groups={{0,2,4,6,8,10,12,14,16,18,20,22,24,26,28,30,32,34,36,38,40,42,44,46,48,..., dimensions={0} | all-to-all | bytes 786432 | tf_op jit(solution)/shard_map/all_to_all | solution.py:394
  45.0 10.2 %shard_map.115 = (bf16[4,32,1024]{2,1,0:T(8,128)(2,1)}, bf16[4,32,1024]{2,1,0:T(8,128)(2,1)}, bf16[32,48,128]{2,1,0:T(8,128)(2,1)}) custom-call(s32[9]{0:T(128)} %get-tuple-element.31.own, s32[9]{0:T(128)} %copy-done.3, bf16[32,48,128]{2,1,0:T(8,128)(2,1)} %all_to_all.21.qkv_ref, bf16[2,2,200,2048]{3,2,1,0:T(8,128)(2,1)} %keys_ref.1, ...), custom_call_target="tpu_custom_call" | custom-call | tf_op jit(solution)/shard_map/pallas_call | solution.py:334
  55.2 12.9 %all_to_all.22.recv_ref = bf16[32,48,128]{2,1,0:T(8,128)(2,1)S(1)} all-to-all(bf16[32,48,128]{2,1,0:T(8,128)(2,1)} %get-tuple-element.41), channel_id=1, replica_groups={{0,2,4,6,8,10,12,14,16,18,20,22,24,26,28,30,32,34,36,38,40,42,44,46,48,..., dimensions={0} | all-to-all | bytes 786432 | tf_op jit(solution)/shard_map/all_to_all | solution.py:394
  68.2 3.1 %collective-permute-start.3 = (bf16[1,112,128]{2,1,0:T(8,128)(2,1)S(1)}, bf16[1,112,128]{2,1,0:T(8,128)(2,1)S(1)}, u32[]{:S(2)}, u32[]{:S(2)}) collective-permute-start(bf16[1,112,128]{2,1,0:T(8,128)(2,1)S(1)} %shard_map.116), channel_id=1, source_target_pairs={{0,64},{64,0},{128,192},{192,128},{1,65},{65,1},{129,193},{193,129... | collective-permute-start | bytes 86024 | tf_op jit(solution)/shard_map/ppermute | solution.py:463
  71.3 1.3 %collective-permute-done.3 = bf16[1,112,128]{2,1,0:T(8,128)(2,1)S(1)} collective-permute-done((bf16[1,112,128]{2,1,0:T(8,128)(2,1)S(1)}, bf16[1,112,128]{2,1,0:T(8,128)(2,1)S(1)}, u32[]{:S(2)}, u32[]{:S(2)}) %collective-permute-start.3) | collective-permute-done | bytes 28704 | tf_op jit(solution)/shard_map/ppermute | solution.py:463
  72.5 4.6 %collective-permute-start.4 = (bf16[2,112,128]{2,1,0:T(8,128)(2,1)S(1)}, bf16[2,112,128]{2,1,0:T(8,128)(2,1)S(1)}, u32[]{:S(2)}, u32[]{:S(2)}) collective-permute-start(bf16[2,112,128]{2,1,0:T(8,128)(2,1)S(1)} %pad_maximum_fusion.first_ref), channel_id=1, source_target_pairs={{0,192},{64,128},{128,64},{192,0},{1,193},{65,129},{129,65},{193,1... | collective-permute-start | bytes 172040 | tf_op jit(solution)/shard_map/ppermute | solution.py:464
  77.1 1.7 %collective-permute-done.4.second_ref = bf16[2,112,128]{2,1,0:T(8,128)(2,1)S(1)} collective-permute-done((bf16[2,112,128]{2,1,0:T(8,128)(2,1)S(1)}, bf16[2,112,128]{2,1,0:T(8,128)(2,1)S(1)}, u32[]{:S(2)}, u32[]{:S(2)}) %collective-permute-start.4) | collective-permute-done | bytes 57376 | tf_op jit(solution)/shard_map/ppermute | solution.py:464
  78.8 1.3 %shard_map.117 = bf16[32,192,128]{2,1,0:T(8,128)(2,1)} custom-call(bf16[2,112,128]{2,1,0:T(8,128)(2,1)S(1)} %pad_maximum_fusion.first_ref, bf16[2,112,128]{2,1,0:T(8,128)(2,1)S(1)} %collective-permute-done.4.second_ref), custom_call_target="tpu_custom_call" | custom-call | tf_op jit(solution)/shard_map/pallas_call | solution.py:465
  80.1 4.3 %all-to-all-start.3 = ((bf16[32,192,128]{2,1,0:T(8,128)(2,1)}), bf16[32,192,128]{2,1,0:T(8,128)(2,1)S(1)}, u32[]{:S(2)}, u32[]{:S(2)}) async-start(bf16[32,192,128]{2,1,0:T(8,128)(2,1)} %shard_map.117), calls=%async_computation.3 | async-start | bytes 3145728 | tf_op jit(solution)/shard_map/all_to_all | solution.py:394
  84.4 5.6 %collective-permute-start.5 = (bf16[4,32,1024]{2,1,0:T(8,128)(2,1)}, bf16[4,32,1024]{2,1,0:T(8,128)(2,1)S(1)}, u32[]{:S(2)}, u32[]{:S(2)}) collective-permute-start(bf16[4,32,1024]{2,1,0:T(8,128)(2,1)} %get-tuple-element.45), channel_id=1, source_target_pairs={{0,1},{1,0},{2,3},{3,2},{4,5},{5,4},{6,7},{7,6},{8,9},{9,8},{10,11... | collective-permute-start | bytes 786440 | tf_op jit(solution)/shard_map/ppermute | solution.py:448
  90.0 1.4 %collective-permute-done.5.theirs_ref = bf16[4,32,1024]{2,1,0:T(8,128)(2,1)S(1)} collective-permute-done((bf16[4,32,1024]{2,1,0:T(8,128)(2,1)}, bf16[4,32,1024]{2,1,0:T(8,128)(2,1)S(1)}, u32[]{:S(2)}, u32[]{:S(2)}) %collective-permute-start.5) | collective-permute-done | bytes 262176 | tf_op jit(solution)/shard_map/ppermute | solution.py:448
  91.4 0.9 copy-done.2
  92.3 0.8 shard_map.118
  93.2 7.4 %all-to-all-done.3.recv_ref = bf16[32,192,128]{2,1,0:T(8,128)(2,1)S(1)} async-done(((bf16[32,192,128]{2,1,0:T(8,128)(2,1)}), bf16[32,192,128]{2,1,0:T(8,128)(2,1)S(1)}, u32[]{:S(2)}, u32[]{:S(2)}) %all-to-all-start.3) | async-done | bytes 1572896 | tf_op jit(solution)/shard_map/all_to_all | solution.py:394
  100.5 1.0 shard_map.119
  101.6 7.0 %collective-permute-start.6 = (bf16[80,3328]{1,0:T(8,128)(2,1)S(1)}, bf16[80,3328]{1,0:T(8,128)(2,1)S(1)}, u32[]{:S(2)}, u32[]{:S(2)}) collective-permute-start(bf16[80,3328]{1,0:T(8,128)(2,1)S(1)} %get-tuple-element.50), channel_id=1, source_target_pairs={{0,1},{1,0},{2,3},{3,2},{4,5},{5,4},{6,7},{7,6},{8,9},{9,8},{10,11... | collective-permute-start | bytes 1597448 | tf_op jit(solution)/shard_map/ppermute | solution.py:478
  108.5 1.2 %shard_map.120.in_ref = f32[64,6144]{1,0:T(8,128)} custom-call(s32[1]{0:T(128)S(6)} %select_n.7.core, bf16[8,256,384]{2,1,0:T(8,128)(2,1)S(1)} %get-tuple-element.53.d_pre_ref, bf16[64,256]{1,0:T(8,128)(2,1)S(1)} %get-tuple-element.54.scaled_ref), custom_call_target="tpu_custom_call" | custom-call | tf_op jit(solution)/shard_map/pallas_call | solution.py:480
  110.1 1.5 %shard_map.121 = (bf16[64,64]{1,0:T(8,128)(2,1)}, f32[1,64]{1,0:T(1,128)}, f32[64,6144]{1,0:T(8,128)}) custom-call(s32[1]{0:T(128)S(6)} %select_n.7.core, bf16[80,3328]{1,0:T(8,128)(2,1)S(1)} %collective-permute-done.6.recv_ref, f32[144,128]{1,0:T(8,128)S(1)} %get-tuple-element.51.small_ref, ...), custom_call_target="tpu_custom_call", output_to_operand_aliasing={{2}: (5, {})} | custom-call | tf_op jit(solution)/shard_map/pallas_call | solution.py:488
  (15 shorter events, 0.7 us)
Async XLA Ops:
  2.8 6.6 %collective-permute-start = (bf16[80,3072]{1,0:T(8,128)(2,1)}, bf16[80,3072]{1,0:T(8,128)(2,1)S(1)}, u32[]{:S(2)}, u32[]{:S(2)}) collective-permute-start(bf16[80,3072]{1,0:T(8,128)(2,1)} %get-tuple-element.32), channel_id=1, source_target_pairs={{0,1},{1,0},{2,3},{3,2},{4,5},{5,4},{6,7},{7,6},{8,9},{9,8},{10,11... | collective-permute-start | bytes 1474568 | tf_op jit(solution)/shard_map/ppermute | solution.py:408
  6.1 3.7 %copy-start.1 = (bf16[80,3072]{1,0:T(8,128)(2,1)S(1)}, bf16[80,3072]{1,0:T(8,128)(2,1)}, u32[]{:S(2)}) copy-start(bf16[80,3072]{1,0:T(8,128)(2,1)} %get-tuple-element.34.mine_ref) | copy-start | bytes 1474564
  6.2 3.2 %collective-permute-start.1 = (s32[9]{0:T(128)}, s32[9]{0:T(128)S(1)}, u32[]{:S(2)}, u32[]{:S(2)}) collective-permute-start(s32[9]{0:T(128)} %get-tuple-element.31.own), channel_id=1, source_target_pairs={{0,1},{1,0},{2,3},{3,2},{4,5},{5,4},{6,7},{7,6},{8,9},{9,8},{10,11... | collective-permute-start | bytes 116 | tf_op jit(solution)/shard_map/ppermute | solution.py:408
  9.4 21.5 %copy-start.3 = (s32[9]{0:T(128)}, s32[9]{0:T(128)S(1)}, u32[]{:S(2)}) copy-start(s32[9]{0:T(128)S(1)} %collective-permute-done.1.oth) | copy-start | bytes 112
  9.4 35.6 %collective-permute-start.2 = (bf16[4,3,200,1024]{3,2,1,0:T(8,128)(2,1)}, bf16[4,3,200,1024]{3,2,1,0:T(8,128)(2,1)}, u32[]{:S(2)}, u32[]{:S(2)}) collective-permute-start(bf16[4,3,200,1024]{3,2,1,0:T(8,128)(2,1)} %shard_map.112), channel_id=1, source_target_pairs={{0,1},{1,0},{2,3},{3,2},{4,5},{5,4},{6,7},{7,6},{8,9},{9,8},{10,11... | collective-permute-start | bytes 14745608 | tf_op jit(solution)/shard_map/ppermute | solution.py:425
  68.2 4.3 %collective-permute-start.3 = (bf16[1,112,128]{2,1,0:T(8,128)(2,1)S(1)}, bf16[1,112,128]{2,1,0:T(8,128)(2,1)S(1)}, u32[]{:S(2)}, u32[]{:S(2)}) collective-permute-start(bf16[1,112,128]{2,1,0:T(8,128)(2,1)S(1)} %shard_map.116), channel_id=1, source_target_pairs={{0,64},{64,0},{128,192},{192,128},{1,65},{65,1},{129,193},{193,129... | collective-permute-start | bytes 86024 | tf_op jit(solution)/shard_map/ppermute | solution.py:463
  72.5 6.2 %collective-permute-start.4 = (bf16[2,112,128]{2,1,0:T(8,128)(2,1)S(1)}, bf16[2,112,128]{2,1,0:T(8,128)(2,1)S(1)}, u32[]{:S(2)}, u32[]{:S(2)}) collective-permute-start(bf16[2,112,128]{2,1,0:T(8,128)(2,1)S(1)} %pad_maximum_fusion.first_ref), channel_id=1, source_target_pairs={{0,192},{64,128},{128,64},{192,0},{1,193},{65,129},{129,65},{193,1... | collective-permute-start | bytes 172040 | tf_op jit(solution)/shard_map/ppermute | solution.py:464
  80.1 20.4 %copy-start = (bf16[32,48,128]{2,1,0:T(8,128)(2,1)S(1)}, bf16[32,48,128]{2,1,0:T(8,128)(2,1)}, u32[]{:S(2)}) copy-start(bf16[32,48,128]{2,1,0:T(8,128)(2,1)} %all_to_all.21.qkv_ref) | copy-start | bytes 1179652
  80.1 20.4 %all-to-all-start.3 = ((bf16[32,192,128]{2,1,0:T(8,128)(2,1)}), bf16[32,192,128]{2,1,0:T(8,128)(2,1)S(1)}, u32[]{:S(2)}, u32[]{:S(2)}) async-start(bf16[32,192,128]{2,1,0:T(8,128)(2,1)} %shard_map.117), calls=%async_computation.3 | async-start | bytes 3145728 | tf_op jit(solution)/shard_map/all_to_all | solution.py:394
  84.4 7.0 %collective-permute-start.5 = (bf16[4,32,1024]{2,1,0:T(8,128)(2,1)}, bf16[4,32,1024]{2,1,0:T(8,128)(2,1)S(1)}, u32[]{:S(2)}, u32[]{:S(2)}) collective-permute-start(bf16[4,32,1024]{2,1,0:T(8,128)(2,1)} %get-tuple-element.45), channel_id=1, source_target_pairs={{0,1},{1,0},{2,3},{3,2},{4,5},{5,4},{6,7},{7,6},{8,9},{9,8},{10,11... | collective-permute-start | bytes 786440 | tf_op jit(solution)/shard_map/ppermute | solution.py:448
  91.4 0.9 copy-start.2
  101.6 8.5 %collective-permute-start.6 = (bf16[80,3328]{1,0:T(8,128)(2,1)S(1)}, bf16[80,3328]{1,0:T(8,128)(2,1)S(1)}, u32[]{:S(2)}, u32[]{:S(2)}) collective-permute-start(bf16[80,3328]{1,0:T(8,128)(2,1)S(1)} %get-tuple-element.50), channel_id=1, source_target_pairs={{0,1},{1,0},{2,3},{3,2},{4,5},{5,4},{6,7},{7,6},{8,9},{9,8},{10,11... | collective-permute-start | bytes 1597448 | tf_op jit(solution)/shard_map/ppermute | solution.py:478

commit v5 on v4

--- a/solution.py
+++ b/solution.py
@@ -238,11 +238,25 @@
     out_ref[0, CHUNK:] = pair_ref[...]
 
 
-def spread(first_ref, second_ref, out_ref):
-    for k in range(CHIPS):
-        for g in range(4):
-            ref = first_ref if g < 2 else second_ref
-            out_ref[k, g * CHUNK : (g + 1) * CHUNK] = ref[g % 2, 0:CHUNK]
+def spread(at, chunks_ref, out_hbm, stage, sems):
+    for g in range(2):
+        stage[g * CHUNK : (g + 1) * CHUNK] = chunks_ref[g, 0:CHUNK]
+    copies = [
+        pltpu.make_async_copy(stage, out_hbm.at[k, at : at + 2 * CHUNK], sems.at[k])
+        for k in range(CHIPS)
+    ]
+    for copy in copies:
+        copy.start()
+    for copy in copies:
+        copy.wait()
+
+
+def spread_first(chunks_ref, out_hbm, stage, sems):
+    spread(0, chunks_ref, out_hbm, stage, sems)
+
+
+def spread_second(chunks_ref, in_hbm, out_hbm, stage, sems):
+    spread(2 * CHUNK, chunks_ref, out_hbm, stage, sems)
 
 
 def weight_grads(
@@ -462,7 +476,19 @@
     (chunk,) = call(finish_grad, [((1, CHUNK + ROWS, 128), BF16)], [VMEM] * 3)(grads, rate, pair)
     first = jnp.concatenate([chunk, lax.ppermute(chunk, "dp", [(g, g ^ 1) for g in range(4)])])
     second = lax.ppermute(first, "dp", [(g, g ^ 3) for g in range(4)])
-    (d_pre,) = call(spread, [((CHIPS, 4 * CHUNK, 128), BF16)], [VMEM] * 2)(first, second)
+    spaces = dict(
+        out_shape=jax.ShapeDtypeStruct((CHIPS, 4 * CHUNK, 128), BF16),
+        out_specs=any_space,
+        scratch_shapes=[
+            pltpu.VMEM((2 * CHUNK, 128), BF16),
+            pltpu.SemaphoreType.DMA((CHIPS,)),
+        ],
+        compiler_params=PARAMS,
+    )
+    d_pre = pl.pallas_call(spread_first, in_specs=[VMEM], **spaces)(first)
+    d_pre = pl.pallas_call(
+        spread_second, in_specs=[VMEM, any_space], input_output_aliases={1: 0}, **spaces
+    )(second, d_pre)
     d_pre, context = lax.optimization_barrier((exchange(d_pre), context))
     send, small, blocks, scaled = call(
         weight_grads,

time: 112 us -> 112 us (level)
  waiting for transfers between devices: 12 us -> 10.8 us
    ppermute x1, waiting for transfers between devices: 1.67 us -> 0.52 us  [shards(): second = lax.ppermute(first, 'dp', [(g, g ^ 3) for g in range(4)])]
    pallas_call x1 -> x2, Pallas kernels: 1.35 us -> 2.28 us  [the longest x1 1.14 us: shards(): pl.pallas_call(spread_second, in_specs=[VMEM, any_space], input_output_al...]
  transfers between devices with their start and end apart: 8 -> 8, of which waited for: 5 -> 5; matrix products, arithmetic and copies ran while one was open for 0% -> 0% of each run, Pallas kernels for 5% -> 6%
where the time goes in v5:
time: 112 us; the launch traced here: 111 us
  blocking collectives  47.5 us (42%)
  starting transfers between devices  28.4 us (25%)
  Pallas kernels  23 us (21%)
  waiting for transfers between devices  10.8 us (10%)
    all_to_all x3, blocking collectives, exchange(): lax.all_to_all(x, 'passage', 0, 0, tiled=True, axis_index_groups=same_core)  47.5 us
    pallas_call x1, Pallas kernels, attention(): pl.pallas_call(attend, out_shape=[jax.ShapeDtypeStruct((4, QLEN, HALF), B...  10.2 us
    all_to_all x1, waiting for transfers between devices, exchange(): lax.all_to_all(x, 'passage', 0, 0, tiled=True, axis_index_groups=same_core)  7.39 us
    ppermute x1, starting transfers between devices, shards(): recv = lax.ppermute(send, 'passage', swap)  6.94 us
    ppermute x1, starting transfers between devices, shards(): ctx_mine = lax.ppermute(ctx_oth, 'passage', swap)  5.58 us
    ppermute x1, starting transfers between devices, shards(): second = lax.ppermute(first, 'dp', [(g, g ^ 3) for g in range(4)])  4.56 us
    all_to_all x1, starting transfers between devices, exchange(): lax.all_to_all(x, 'passage', 0, 0, tiled=True, axis_index_groups=same_core)  4.33 us
    ppermute x1, starting transfers between devices, shards(): lax.ppermute(sent, 'passage', swap)  3.33 us
  transfers between devices with their start and end apart: 8, of which 5 were waited for; matrix products, arithmetic and copies ran while one was open for 0% of the time, Pallas kernels for 6%

profile of v5, /device:TPU:1, one launch (start us, length us, event | category | flops | bytes accessed | tf_op | source)
XLA Modules:
  0.0 111.4 jit_solution(9606199462029191438)
XLA Ops:
  0.6 2.2 %shard_map.111 = (bf16[80,3072]{1,0:T(8,128)(2,1)}, bf16[80,3072]{1,0:T(8,128)(2,1)}, s32[9]{0:T(128)}) custom-call(s32[1]{0:T(128)S(6)} %select_n.7.core, s32[2,2]{1,0:T(2,128)} %length.1, s32[2,1,2]{2,1,0:T(1,128)} %owner.1, bf16[64,6144]{1,0:T(8,128)(2,1)} %w_ref.1, bf16[64,64]{1,0:T(8,128)(2,1)} %bitcast.7, bf16[1,64]{1,0:T(2,128)(2,1)} %bitcast.8), custom_call_target="tpu_custom_call" | custom-call | tf_op jit(solution)/shard_map/pallas_call | solution.py:414
  2.8 3.3 %collective-permute-start = (bf16[80,3072]{1,0:T(8,128)(2,1)}, bf16[80,3072]{1,0:T(8,128)(2,1)S(1)}, u32[]{:S(2)}, u32[]{:S(2)}) collective-permute-start(bf16[80,3072]{1,0:T(8,128)(2,1)} %get-tuple-element.32), channel_id=1, source_target_pairs={{0,1},{1,0},{2,3},{3,2},{4,5},{5,4},{6,7},{7,6},{8,9},{9,8},{10,11... | collective-permute-start | bytes 1474568 | tf_op jit(solution)/shard_map/ppermute | solution.py:422
  6.3 3.1 %shard_map.112 = bf16[4,3,200,1024]{3,2,1,0:T(8,128)(2,1)} custom-call(s32[1]{0:T(128)S(6)} %select_n.7.core, bf16[2,2,200,2048]{3,2,1,0:T(8,128)(2,1)} %keys_ref.1, bf16[2,2,200,2048]{3,2,1,0:T(8,128)(2,1)} %values_ref.1, bf16[2,2,32,2048]{3,2,1,0:T(8,128)(2,1)} %d_ref.1), custom_call_target="tpu_custom_call" | custom-call | tf_op jit(solution)/shard_map/pallas_call | solution.py:426
  9.4 0.5 collective-permute-start.2
  10.2 20.4 %all_to_all.20.part_ref = f32[32,56,128]{2,1,0:T(8,128)S(1)} all-to-all(f32[32,56,128]{2,1,0:T(8,128)S(1)} %get-tuple-element.38), channel_id=1, replica_groups={{0,2,4,6,8,10,12,14,16,18,20,22,24,26,28,30,32,34,36,38,40,42,44,46,48,..., dimensions={0} | all-to-all | bytes 1835008 | tf_op jit(solution)/shard_map/all_to_all | solution.py:408
  30.9 14.1 %all_to_all.21.qkv_ref = bf16[32,48,128]{2,1,0:T(8,128)(2,1)} all-to-all(bf16[32,48,128]{2,1,0:T(8,128)(2,1)S(1)} %get-tuple-element.39), channel_id=1, replica_groups={{0,2,4,6,8,10,12,14,16,18,20,22,24,26,28,30,32,34,36,38,40,42,44,46,48,..., dimensions={0} | all-to-all | bytes 786432 | tf_op jit(solution)/shard_map/all_to_all | solution.py:408
  45.0 10.2 %shard_map.115 = (bf16[4,32,1024]{2,1,0:T(8,128)(2,1)}, bf16[4,32,1024]{2,1,0:T(8,128)(2,1)}, bf16[32,48,128]{2,1,0:T(8,128)(2,1)}) custom-call(s32[9]{0:T(128)} %get-tuple-element.31.own, s32[9]{0:T(128)} %copy-done.3, bf16[32,48,128]{2,1,0:T(8,128)(2,1)} %all_to_all.21.qkv_ref, bf16[2,2,200,2048]{3,2,1,0:T(8,128)(2,1)} %keys_ref.1, ...), custom_call_target="tpu_custom_call" | custom-call | tf_op jit(solution)/shard_map/pallas_call | solution.py:348
  55.2 12.9 %all_to_all.22.recv_ref = bf16[32,48,128]{2,1,0:T(8,128)(2,1)S(1)} all-to-all(bf16[32,48,128]{2,1,0:T(8,128)(2,1)} %get-tuple-element.41), channel_id=1, replica_groups={{0,2,4,6,8,10,12,14,16,18,20,22,24,26,28,30,32,34,36,38,40,42,44,46,48,..., dimensions={0} | all-to-all | bytes 786432 | tf_op jit(solution)/shard_map/all_to_all | solution.py:408
  68.2 3.1 %collective-permute-start.3 = (bf16[1,112,128]{2,1,0:T(8,128)(2,1)S(1)}, bf16[1,112,128]{2,1,0:T(8,128)(2,1)S(1)}, u32[]{:S(2)}, u32[]{:S(2)}) collective-permute-start(bf16[1,112,128]{2,1,0:T(8,128)(2,1)S(1)} %shard_map.116), channel_id=1, source_target_pairs={{0,64},{64,0},{128,192},{192,128},{1,65},{65,1},{129,193},{193,129... | collective-permute-start | bytes 86024 | tf_op jit(solution)/shard_map/ppermute | solution.py:477
  71.3 1.3 %collective-permute-done.3 = bf16[1,112,128]{2,1,0:T(8,128)(2,1)S(1)} collective-permute-done((bf16[1,112,128]{2,1,0:T(8,128)(2,1)S(1)}, bf16[1,112,128]{2,1,0:T(8,128)(2,1)S(1)}, u32[]{:S(2)}, u32[]{:S(2)}) %collective-permute-start.3) | collective-permute-done | bytes 28704 | tf_op jit(solution)/shard_map/ppermute | solution.py:477
  72.5 4.6 %collective-permute-start.4 = (bf16[2,112,128]{2,1,0:T(8,128)(2,1)S(1)}, bf16[2,112,128]{2,1,0:T(8,128)(2,1)S(1)}, u32[]{:S(2)}, u32[]{:S(2)}) collective-permute-start(bf16[2,112,128]{2,1,0:T(8,128)(2,1)S(1)} %pad_maximum_fusion.chunks_ref.first_ref), channel_id=1, source_target_pairs={{0,192},{64,128},{128,64},{192,0},{1,193},{65,129},{129,65},{193,1... | collective-permute-start | bytes 172040 | tf_op jit(solution)/shard_map/ppermute | solution.py:478
  77.1 1.1 %shard_map.117.in_hbm = bf16[32,192,128]{2,1,0:T(8,128)(2,1)} custom-call(bf16[2,112,128]{2,1,0:T(8,128)(2,1)S(1)} %pad_maximum_fusion.chunks_ref.first_ref), custom_call_target="tpu_custom_call" | custom-call | tf_op jit(solution)/shard_map/pallas_call | solution.py:488
  78.2 0.5 collective-permute-done.4.chunks_ref.second_ref
  78.8 1.1 %shard_map.118 = bf16[32,192,128]{2,1,0:T(8,128)(2,1)} custom-call(bf16[2,112,128]{2,1,0:T(8,128)(2,1)S(1)} %collective-permute-done.4.chunks_ref.second_ref, bf16[32,192,128]{2,1,0:T(8,128)(2,1)} %shard_map.117.in_hbm), custom_call_target="tpu_custom_call", output_to_operand_aliasing={{}: (1, {})} | custom-call | tf_op jit(solution)/shard_map/pallas_call | solution.py:489
  79.9 4.3 %all-to-all-start.3 = ((bf16[32,192,128]{2,1,0:T(8,128)(2,1)}), bf16[32,192,128]{2,1,0:T(8,128)(2,1)S(1)}, u32[]{:S(2)}, u32[]{:S(2)}) async-start(bf16[32,192,128]{2,1,0:T(8,128)(2,1)} %shard_map.118), calls=%async_computation.3 | async-start | bytes 3145728 | tf_op jit(solution)/shard_map/all_to_all | solution.py:408
  84.3 5.6 %collective-permute-start.5 = (bf16[4,32,1024]{2,1,0:T(8,128)(2,1)}, bf16[4,32,1024]{2,1,0:T(8,128)(2,1)S(1)}, u32[]{:S(2)}, u32[]{:S(2)}) collective-permute-start(bf16[4,32,1024]{2,1,0:T(8,128)(2,1)} %get-tuple-element.45), channel_id=1, source_target_pairs={{0,1},{1,0},{2,3},{3,2},{4,5},{5,4},{6,7},{7,6},{8,9},{9,8},{10,11... | collective-permute-start | bytes 786440 | tf_op jit(solution)/shard_map/ppermute | solution.py:462
  89.8 1.4 %collective-permute-done.5.theirs_ref = bf16[4,32,1024]{2,1,0:T(8,128)(2,1)S(1)} collective-permute-done((bf16[4,32,1024]{2,1,0:T(8,128)(2,1)}, bf16[4,32,1024]{2,1,0:T(8,128)(2,1)S(1)}, u32[]{:S(2)}, u32[]{:S(2)}) %collective-permute-start.5) | collective-permute-done | bytes 262176 | tf_op jit(solution)/shard_map/ppermute | solution.py:462
  91.2 0.9 copy-done.2
  92.2 0.8 shard_map.119
  93.0 7.4 %all-to-all-done.3.recv_ref = bf16[32,192,128]{2,1,0:T(8,128)(2,1)S(1)} async-done(((bf16[32,192,128]{2,1,0:T(8,128)(2,1)}), bf16[32,192,128]{2,1,0:T(8,128)(2,1)S(1)}, u32[]{:S(2)}, u32[]{:S(2)}) %all-to-all-start.3) | async-done | bytes 1572896 | tf_op jit(solution)/shard_map/all_to_all | solution.py:408
  100.4 1.0 shard_map.120
  101.4 6.9 %collective-permute-start.6 = (bf16[80,3328]{1,0:T(8,128)(2,1)S(1)}, bf16[80,3328]{1,0:T(8,128)(2,1)S(1)}, u32[]{:S(2)}, u32[]{:S(2)}) collective-permute-start(bf16[80,3328]{1,0:T(8,128)(2,1)S(1)} %get-tuple-element.50), channel_id=1, source_target_pairs={{0,1},{1,0},{2,3},{3,2},{4,5},{5,4},{6,7},{7,6},{8,9},{9,8},{10,11... | collective-permute-start | bytes 1597448 | tf_op jit(solution)/shard_map/ppermute | solution.py:504
  108.4 1.2 %shard_map.121.in_ref = f32[64,6144]{1,0:T(8,128)} custom-call(s32[1]{0:T(128)S(6)} %select_n.7.core, bf16[8,256,384]{2,1,0:T(8,128)(2,1)S(1)} %get-tuple-element.53.d_pre_ref, bf16[64,256]{1,0:T(8,128)(2,1)S(1)} %get-tuple-element.54.scaled_ref), custom_call_target="tpu_custom_call" | custom-call | tf_op jit(solution)/shard_map/pallas_call | solution.py:506
  109.9 1.5 %shard_map.122 = (bf16[64,64]{1,0:T(8,128)(2,1)}, f32[1,64]{1,0:T(1,128)}, f32[64,6144]{1,0:T(8,128)}) custom-call(s32[1]{0:T(128)S(6)} %select_n.7.core, bf16[80,3328]{1,0:T(8,128)(2,1)S(1)} %collective-permute-done.6.recv_ref, f32[144,128]{1,0:T(8,128)S(1)} %get-tuple-element.51.small_ref, ...), custom_call_target="tpu_custom_call", output_to_operand_aliasing={{2}: (5, {})} | custom-call | tf_op jit(solution)/shard_map/pallas_call | solution.py:514
  (16 shorter events, 1.1 us)
Async XLA Ops:
  2.8 6.6 %collective-permute-start = (bf16[80,3072]{1,0:T(8,128)(2,1)}, bf16[80,3072]{1,0:T(8,128)(2,1)S(1)}, u32[]{:S(2)}, u32[]{:S(2)}) collective-permute-start(bf16[80,3072]{1,0:T(8,128)(2,1)} %get-tuple-element.32), channel_id=1, source_target_pairs={{0,1},{1,0},{2,3},{3,2},{4,5},{5,4},{6,7},{7,6},{8,9},{9,8},{10,11... | collective-permute-start | bytes 1474568 | tf_op jit(solution)/shard_map/ppermute | solution.py:422
  6.1 3.7 %copy-start.1 = (bf16[80,3072]{1,0:T(8,128)(2,1)S(1)}, bf16[80,3072]{1,0:T(8,128)(2,1)}, u32[]{:S(2)}) copy-start(bf16[80,3072]{1,0:T(8,128)(2,1)} %get-tuple-element.34.mine_ref) | copy-start | bytes 1474564
  6.2 3.2 %collective-permute-start.1 = (s32[9]{0:T(128)}, s32[9]{0:T(128)S(1)}, u32[]{:S(2)}, u32[]{:S(2)}) collective-permute-start(s32[9]{0:T(128)} %get-tuple-element.31.own), channel_id=1, source_target_pairs={{0,1},{1,0},{2,3},{3,2},{4,5},{5,4},{6,7},{7,6},{8,9},{9,8},{10,11... | collective-permute-start | bytes 116 | tf_op jit(solution)/shard_map/ppermute | solution.py:422
  9.4 21.5 %copy-start.3 = (s32[9]{0:T(128)}, s32[9]{0:T(128)S(1)}, u32[]{:S(2)}) copy-start(s32[9]{0:T(128)S(1)} %collective-permute-done.1.oth) | copy-start | bytes 112
  9.4 35.6 %collective-permute-start.2 = (bf16[4,3,200,1024]{3,2,1,0:T(8,128)(2,1)}, bf16[4,3,200,1024]{3,2,1,0:T(8,128)(2,1)}, u32[]{:S(2)}, u32[]{:S(2)}) collective-permute-start(bf16[4,3,200,1024]{3,2,1,0:T(8,128)(2,1)} %shard_map.112), channel_id=1, source_target_pairs={{0,1},{1,0},{2,3},{3,2},{4,5},{5,4},{6,7},{7,6},{8,9},{9,8},{10,11... | collective-permute-start | bytes 14745608 | tf_op jit(solution)/shard_map/ppermute | solution.py:439
  68.2 4.3 %collective-permute-start.3 = (bf16[1,112,128]{2,1,0:T(8,128)(2,1)S(1)}, bf16[1,112,128]{2,1,0:T(8,128)(2,1)S(1)}, u32[]{:S(2)}, u32[]{:S(2)}) collective-permute-start(bf16[1,112,128]{2,1,0:T(8,128)(2,1)S(1)} %shard_map.116), channel_id=1, source_target_pairs={{0,64},{64,0},{128,192},{192,128},{1,65},{65,1},{129,193},{193,129... | collective-permute-start | bytes 86024 | tf_op jit(solution)/shard_map/ppermute | solution.py:477
  72.5 6.2 %collective-permute-start.4 = (bf16[2,112,128]{2,1,0:T(8,128)(2,1)S(1)}, bf16[2,112,128]{2,1,0:T(8,128)(2,1)S(1)}, u32[]{:S(2)}, u32[]{:S(2)}) collective-permute-start(bf16[2,112,128]{2,1,0:T(8,128)(2,1)S(1)} %pad_maximum_fusion.chunks_ref.first_ref), channel_id=1, source_target_pairs={{0,192},{64,128},{128,64},{192,0},{1,193},{65,129},{129,65},{193,1... | collective-permute-start | bytes 172040 | tf_op jit(solution)/shard_map/ppermute | solution.py:478
  79.9 20.5 %copy-start = (bf16[32,48,128]{2,1,0:T(8,128)(2,1)S(1)}, bf16[32,48,128]{2,1,0:T(8,128)(2,1)}, u32[]{:S(2)}) copy-start(bf16[32,48,128]{2,1,0:T(8,128)(2,1)} %all_to_all.21.qkv_ref) | copy-start | bytes 1179652
  79.9 20.4 %all-to-all-start.3 = ((bf16[32,192,128]{2,1,0:T(8,128)(2,1)}), bf16[32,192,128]{2,1,0:T(8,128)(2,1)S(1)}, u32[]{:S(2)}, u32[]{:S(2)}) async-start(bf16[32,192,128]{2,1,0:T(8,128)(2,1)} %shard_map.118), calls=%async_computation.3 | async-start | bytes 3145728 | tf_op jit(solution)/shard_map/all_to_all | solution.py:408
  84.3 7.0 %collective-permute-start.5 = (bf16[4,32,1024]{2,1,0:T(8,128)(2,1)}, bf16[4,32,1024]{2,1,0:T(8,128)(2,1)S(1)}, u32[]{:S(2)}, u32[]{:S(2)}) collective-permute-start(bf16[4,32,1024]{2,1,0:T(8,128)(2,1)} %get-tuple-element.45), channel_id=1, source_target_pairs={{0,1},{1,0},{2,3},{3,2},{4,5},{5,4},{6,7},{7,6},{8,9},{9,8},{10,11... | collective-permute-start | bytes 786440 | tf_op jit(solution)/shard_map/ppermute | solution.py:462
  91.2 0.9 copy-start.2
  101.4 8.5 %collective-permute-start.6 = (bf16[80,3328]{1,0:T(8,128)(2,1)S(1)}, bf16[80,3328]{1,0:T(8,128)(2,1)S(1)}, u32[]{:S(2)}, u32[]{:S(2)}) collective-permute-start(bf16[80,3328]{1,0:T(8,128)(2,1)S(1)} %get-tuple-element.50), channel_id=1, source_target_pairs={{0,1},{1,0},{2,3},{3,2},{4,5},{5,4},{6,7},{7,6},{8,9},{9,8},{10,11... | collective-permute-start | bytes 1597448 | tf_op jit(solution)/shard_map/ppermute | solution.py:504
